TPU v7x, 256 devices: a whole 4x4x8 slice. The times are simulated.
256 devices in a mesh: ha: 4 (over z_hi), wa: 8 (over z_lo, x), hd: 8 (over y, core).
Axes of the slice: x: 4, y: 4, z: 8 (z_hi: 4, z_lo: 2; z = z_hi * 2 + z_lo), core: 2. Of those that a mesh axis runs over, the one named last changes fastest.
Arguments:
- query_in: bfloat16 [4, 8, 256, 3072], P('ha', 'wa', 'hd'), may hold values from -6 to 6
- key_in: bfloat16 [4, 8, 256, 3072], P('ha', 'wa', 'hd'), may hold values from -6 to 6
- value_in: bfloat16 [4, 8, 256, 3072], P('ha', 'wa', 'hd'), may hold values from -6 to 6
- out_fwd: bfloat16 [4, 8, 256, 3072], P('ha', 'wa', 'hd'), may hold values from -6 to 6
- grad_out: bfloat16 [4, 8, 256, 3072], P('ha', 'wa', 'hd'), may hold values from -6 to 6
- log_norm: float32 [4, 8, 256, 24], P('ha', 'wa', 'hd'), may hold values from 4 to 6
Outputs:
- grad_query: bfloat16 [4, 8, 256, 3072], P('ha', 'wa', 'hd')
- grad_key: bfloat16 [4, 8, 256, 3072], P('ha', 'wa', 'hd')
- grad_value: bfloat16 [4, 8, 256, 3072], P('ha', 'wa', 'hd')
All inputs are finite; a program needn't handle non-finite values.
Results may differ from a plain program's by a relative error of at most 0.009.
Values may be sent and summed in bfloat16 or wider, within the bound.
A program may use at most 64 MiB of HBM per device.

v0:
```python
import jax
import jax.numpy as jnp
from jax import lax
from jax.sharding import PartitionSpec as P

HD = 128


def padded(block, sides, width):
    for axis, dim in sides:
        count = lax.axis_size(axis)
        forward = [(i, i + 1) for i in range(count - 1)]
        backward = [(target, source) for source, target in forward]
        low = lax.ppermute(
            lax.slice_in_dim(block, block.shape[dim] - width, None, axis=dim), axis, forward
        )
        high = lax.ppermute(lax.slice_in_dim(block, 0, width, axis=dim), axis, backward)
        block = jnp.concatenate([low, block, high], axis=dim)
    return block


def passed_along(array, axis, by):
    length = lax.axis_size(axis)
    pairs = [(i, i + by) for i in range(length) if 0 <= i + by < length]
    return lax.ppermute(array, axis, pairs)


def split_heads(block, heads_loc):
    return block.reshape(block.shape[0], block.shape[1], block.shape[2], heads_loc, HD)


def tile_valid(row_off, col_off, rows_h, rows_w):
    glob_h = lax.axis_index("ha") * rows_h + jnp.arange(rows_h, dtype=jnp.int32) + row_off - 1
    glob_w = lax.axis_index("wa") * rows_w + jnp.arange(rows_w, dtype=jnp.int32) + col_off - 1
    inside_h = (glob_h >= 0) & (glob_h < rows_h * lax.axis_size("ha"))
    inside_w = (glob_w >= 0) & (glob_w < rows_w * lax.axis_size("wa"))
    return (inside_h[:, None] & inside_w[None, :]).astype(jnp.float32)


def pair_terms(query_tiles, grad_tiles, norm_rows, dot_rows, key_tiles, value_tiles, valid):
    softmax_scale = HD ** (-0.5)
    scores = (
        jnp.einsum("abqhd,abkhd->abhqk", query_tiles, key_tiles, preferred_element_type=jnp.float32)
        * softmax_scale
    )
    probs = jnp.exp(scores - norm_rows[..., None]) * valid[:, :, None, None, None]
    grad_probs = jnp.einsum(
        "abqhd,abkhd->abhqk", grad_tiles, value_tiles, preferred_element_type=jnp.float32
    )
    grad_scores = (probs * (grad_probs - dot_rows[..., None]) * softmax_scale).astype(jnp.bfloat16)
    return (probs.astype(jnp.bfloat16), grad_scores)


def per_device(query_in, key_in, value_in, out_fwd, grad_out, log_norm):
    rows_h, rows_w = (query_in.shape[0], query_in.shape[1])
    heads_all = query_in.shape[3] // HD
    heads_loc = heads_all // lax.axis_size("hd")
    query_loc, key_loc, value_loc, out_loc, grad_loc = (
        lax.all_to_all(query_in, "hd", split_axis=3, concat_axis=2, tiled=True),
        lax.all_to_all(key_in, "hd", split_axis=3, concat_axis=2, tiled=True),
        lax.all_to_all(value_in, "hd", split_axis=3, concat_axis=2, tiled=True),
        lax.all_to_all(out_fwd, "hd", split_axis=3, concat_axis=2, tiled=True),
        lax.all_to_all(grad_out, "hd", split_axis=3, concat_axis=2, tiled=True),
    )
    norm_loc = lax.all_to_all(log_norm, "hd", split_axis=3, concat_axis=2, tiled=True)
    products = grad_loc.astype(jnp.float32) * out_loc.astype(jnp.float32)
    dots_loc = jnp.sum(split_heads(products, heads_loc), axis=-1)
    chan_loc = query_loc.shape[3]
    tile_len = query_loc.shape[2]
    query_heads = split_heads(query_loc, heads_loc)
    grad_heads = split_heads(grad_loc, heads_loc)
    norm_rows = norm_loc.transpose(0, 1, 3, 2)
    dot_rows = dots_loc.transpose(0, 1, 3, 2)
    kv_ext = padded(jnp.concatenate((key_loc, value_loc), axis=3), (("ha", 0), ("wa", 1)), 1)
    grad_q = jnp.zeros(query_heads.shape, jnp.float32)
    grads_ext = jnp.zeros((rows_h + 2, rows_w + 2, tile_len, 2 * chan_loc), jnp.float32)
    for row_off in range(3):
        for col_off in range(3):
            window = kv_ext[row_off : row_off + rows_h, col_off : col_off + rows_w]
            key_tiles = split_heads(window[..., :chan_loc], heads_loc)
            value_tiles = split_heads(window[..., chan_loc:], heads_loc)
            valid = tile_valid(row_off, col_off, rows_h, rows_w)
            probs_bf, grad_scores = pair_terms(
                query_heads, grad_heads, norm_rows, dot_rows, key_tiles, value_tiles, valid
            )
            grad_q = grad_q + jnp.einsum(
                "abhqk,abkhd->abqhd", grad_scores, key_tiles, preferred_element_type=jnp.float32
            )
            key_part = jnp.einsum(
                "abhqk,abqhd->abkhd", grad_scores, query_heads, preferred_element_type=jnp.float32
            )
            value_part = jnp.einsum(
                "abhqk,abqhd->abkhd", probs_bf, grad_heads, preferred_element_type=jnp.float32
            )
            both_parts = jnp.concatenate(
                (
                    key_part.reshape(rows_h, rows_w, tile_len, chan_loc),
                    value_part.reshape(rows_h, rows_w, tile_len, chan_loc),
                ),
                axis=3,
            )
            grads_ext = grads_ext.at[row_off : row_off + rows_h, col_off : col_off + rows_w].add(
                both_parts
            )
    left_rim = passed_along(grads_ext[:, 0], "wa", -1)
    right_rim = passed_along(grads_ext[:, rows_w + 1], "wa", 1)
    middle = grads_ext[:, 1 : rows_w + 1]
    middle = middle.at[:, rows_w - 1].add(left_rim)
    middle = middle.at[:, 0].add(right_rim)
    low_rim = passed_along(middle[0].astype(jnp.bfloat16), "ha", -1).astype(jnp.float32)
    high_rim = passed_along(middle[rows_h + 1], "ha", 1)
    own_grads = middle[1 : rows_h + 1]
    own_grads = own_grads.at[rows_h - 1].add(low_rim)
    own_grads = own_grads.at[0].add(high_rim)
    grad_k = own_grads[..., :chan_loc].astype(jnp.bfloat16)
    grad_v = own_grads[..., chan_loc:].astype(jnp.bfloat16)
    grad_q = grad_q.reshape(rows_h, rows_w, tile_len, chan_loc).astype(jnp.bfloat16)
    grad_query, grad_key, grad_value = (
        lax.all_to_all(grad_q, "hd", split_axis=2, concat_axis=3, tiled=True),
        lax.all_to_all(grad_k, "hd", split_axis=2, concat_axis=3, tiled=True),
        lax.all_to_all(grad_v, "hd", split_axis=2, concat_axis=3, tiled=True),
    )
    return (grad_query, grad_key, grad_value)


def solution(mesh):
    in_specs = (
        P("ha", "wa", "hd", None),
        P("ha", "wa", "hd", None),
        P("ha", "wa", "hd", None),
        P("ha", "wa", "hd", None),
        P("ha", "wa", "hd", None),
        P("ha", "wa", "hd", None),
    )
    out_specs = (P("ha", "wa", "hd", None), P("ha", "wa", "hd", None), P("ha", "wa", "hd", None))
    return jax.shard_map(
        per_device, mesh=mesh, in_specs=in_specs, out_specs=out_specs, check_vma=False
    )
```

profile of v0, /device:TPU:96, one launch (start us, length us, event | category | flops | bytes accessed | tf_op | source)
XLA Modules:
  0.0 393.9 jit_solution(1404150383155522124)
XLA Ops:
  0.6 4.5 %all-to-all-start.3 = ((f32[1,1,32,24]{2,1,0,3:T(1,128)}), f32[1,1,32,24]{2,1,0,3:T(1,128)S(1)}, u32[]{:S(2)}, u32[]{:S(2)}) async-start(f32[1,1,32,24]{2,1,0,3:T(1,128)} %bitcast.446), calls=%async_computation.3 | async-start | bytes 24576 | tf_op jit(solution)/shard_map/all_to_all | solution.py:65
  5.1 3.3 copy.588
  9.0 17.0 %reduce.35 = bf16[3072,32]{1,0:T(8,128)(2,1)S(1)} reduce(bf16[3072,1,1,32]{3,2,1,0:T(2,128)(2,1)S(1)} %bitcast.355, bf16[]{:T(256)} %broadcast.381), dimensions={1,2}, to_apply=%bitcast.254.reduce_sub_computation | reduce | bytes 393218
  25.9 1.4 reshape.1185
  27.3 5.0 %all-to-all-start = ((bf16[8,2,6144]{2,1,0:T(2,128)(2,1)}), bf16[8,2,6144]{2,1,0:T(2,128)(2,1)S(1)}, u32[]{:S(2)}, u32[]{:S(2)}) async-start(bf16[8,2,6144]{2,1,0:T(2,128)(2,1)} %reshape.1185), calls=%async_computation | async-start | bytes 393216 | tf_op jit(solution)/shard_map/all_to_all | solution.py:60
  32.4 1.8 copy.591
  34.2 17.0 %reduce.34 = bf16[3072,32]{1,0:T(8,128)(2,1)S(1)} reduce(bf16[3072,1,1,32]{3,2,1,0:T(2,128)(2,1)S(1)} %bitcast.361, bf16[]{:T(256)} %broadcast.381), dimensions={1,2}, to_apply=%bitcast.252.reduce_sub_computation | reduce | bytes 393218
  51.2 1.4 reshape.1183
  52.6 5.0 %all-to-all-start.1 = ((bf16[8,2,6144]{2,1,0:T(2,128)(2,1)}), bf16[8,2,6144]{2,1,0:T(2,128)(2,1)S(1)}, u32[]{:S(2)}, u32[]{:S(2)}) async-start(bf16[8,2,6144]{2,1,0:T(2,128)(2,1)} %reshape.1183), calls=%async_computation.1 | async-start | bytes 393216 | tf_op jit(solution)/shard_map/all_to_all | solution.py:61
  57.7 1.8 copy.595
  59.5 17.0 %reduce.36 = bf16[3072,32]{1,0:T(8,128)(2,1)S(1)} reduce(bf16[3072,1,1,32]{3,2,1,0:T(2,128)(2,1)S(1)} %bitcast.362, bf16[]{:T(256)} %broadcast.381), dimensions={1,2}, to_apply=%bitcast.256.reduce_sub_computation | reduce | bytes 393218
  76.5 1.4 reshape.1187
  77.9 5.1 %all-to-all-start.2 = ((bf16[8,2,6144]{2,1,0:T(2,128)(2,1)}), bf16[8,2,6144]{2,1,0:T(2,128)(2,1)S(1)}, u32[]{:S(2)}, u32[]{:S(2)}) async-start(bf16[8,2,6144]{2,1,0:T(2,128)(2,1)} %reshape.1187), calls=%async_computation.2 | async-start | bytes 393216 | tf_op jit(solution)/shard_map/all_to_all | solution.py:59
  83.1 1.8 copy.603
  84.9 17.0 %reduce.37 = bf16[3072,32]{1,0:T(8,128)(2,1)S(1)} reduce(bf16[3072,1,1,32]{3,2,1,0:T(2,128)(2,1)S(1)} %bitcast.363, bf16[]{:T(256)} %broadcast.381), dimensions={1,2}, to_apply=%bitcast.258.reduce_sub_computation | reduce | bytes 393218
  101.9 1.4 reshape.1189
  103.3 1.8 copy.608
  105.1 29.0 %reduce.38 = bf16[3072,32]{1,0:T(8,128)(2,1)S(1)} reduce(bf16[3072,1,1,32]{3,2,1,0:T(2,128)(2,1)S(1)} %bitcast.364, bf16[]{:T(256)} %broadcast.381), dimensions={1,2}, to_apply=%bitcast.260.reduce_sub_computation | reduce | bytes 393218
  134.1 1.4 reshape.1191
  135.5 4.8 %all-to-all-start.4 = ((bf16[8,2,6144]{2,1,0:T(2,128)(2,1)}), bf16[8,2,6144]{2,1,0:T(2,128)(2,1)S(1)}, u32[]{:S(2)}, u32[]{:S(2)}) async-start(bf16[8,2,6144]{2,1,0:T(2,128)(2,1)} %reshape.1189), calls=%async_computation.4 | async-start | bytes 393216 | tf_op jit(solution)/shard_map/all_to_all | solution.py:63
  141.7 5.5 %all-to-all-done.4 = bf16[8,2,6144]{2,1,0:T(2,128)(2,1)S(1)} async-done(((bf16[8,2,6144]{2,1,0:T(2,128)(2,1)}), bf16[8,2,6144]{2,1,0:T(2,128)(2,1)S(1)}, u32[]{:S(2)}, u32[]{:S(2)}) %all-to-all-start.4) | async-done | bytes 196640 | tf_op jit(solution)/shard_map/all_to_all | solution.py:63
  147.1 4.0 %all-to-all-start.5 = ((bf16[8,2,6144]{2,1,0:T(2,128)(2,1)}), bf16[8,2,6144]{2,1,0:T(2,128)(2,1)}, u32[]{:S(2)}, u32[]{:S(2)}) async-start(bf16[8,2,6144]{2,1,0:T(2,128)(2,1)} %reshape.1191), calls=%async_computation.5 | async-start | bytes 393216 | tf_op jit(solution)/shard_map/all_to_all | solution.py:62
  152.8 1.4 copy.589
  155.1 1.4 copy.592
  157.4 5.5 %collective-permute-start = (bf16[1,1,256,768]{3,2,1,0:T(8,128)(2,1)}, bf16[1,1,256,768]{3,2,1,0:T(8,128)(2,1)S(1)}, u32[]{:S(2)}, u32[]{:S(2)}) collective-permute-start(bf16[1,1,256,768]{3,2,1,0:T(8,128)(2,1)} %pad_maximum_fusion.1), channel_id=1, source_target_pairs={{0,64},{64,128},{128,192},{1,65},{65,129},{129,193},{2,66},{66,130... | collective-permute-start | bytes 1179656 | tf_op jit(solution)/shard_map/ppermute | solution.py:14
  162.9 1.9 collective-permute-start.1
  167.2 1.4 copy.596
  169.8 1.4 copy.604
  171.5 2.3 reshape.1192
  173.8 1.4 copy.609
  179.8 6.3 %collective-permute-done.1 = bf16[1,1,256,768]{3,2,1,0:T(8,128)(2,1)S(1)} collective-permute-done((bf16[1,1,256,768]{3,2,1,0:T(8,128)(2,1)}, bf16[1,1,256,768]{3,2,1,0:T(8,128)(2,1)S(1)}, u32[]{:S(2)}, u32[]{:S(2)}) %collective-permute-start.1) | collective-permute-done | bytes 393248 | tf_op jit(solution)/shard_map/ppermute | solution.py:17
  186.1 1.2 pad_maximum_fusion
  187.3 3.4 collective-permute-start.2
  190.7 4.6 %collective-permute-start.3 = (bf16[3,1,256,768]{3,2,1,0:T(8,128)(2,1)}, bf16[3,1,256,768]{3,2,1,0:T(8,128)(2,1)}, u32[]{:S(2)}, u32[]{:S(2)}) collective-permute-start(bf16[3,1,256,768]{3,2,1,0:T(8,128)(2,1)} %pad_maximum_fusion), channel_id=1, source_target_pairs={{8,0},{16,8},{24,16},{32,24},{40,32},{48,40},{56,48},{9,1},{17,9},... | collective-permute-start | bytes 3538952 | tf_op jit(solution)/shard_map/ppermute | solution.py:17
  202.2 16.6 %collective-permute-done.2 = bf16[3,1,256,768]{3,2,1,0:T(8,128)(2,1)} collective-permute-done((bf16[3,1,256,768]{3,2,1,0:T(8,128)(2,1)}, bf16[3,1,256,768]{3,2,1,0:T(8,128)(2,1)}, u32[]{:S(2)}, u32[]{:S(2)}) %collective-permute-start.2) | collective-permute-done | bytes 1179680 | tf_op jit(solution)/shard_map/ppermute | solution.py:14
  218.7 2.3 fusion.93
  224.6 2.3 fusion.92
  235.7 1.8 copy.641
  239.8 1.9 copy.686
  243.7 1.8 copy.647
  249.1 1.9 copy.690
  251.0 1.9 copy.691
  255.2 1.1 fusion.73
  257.6 1.2 copy.698
  258.8 1.9 copy.699
  260.7 1.9 select_maximum_fusion
  262.6 1.5 fusion.71
  264.2 2.0 fusion.62
  269.5 3.8 collective-permute-start.4
  273.2 2.3 collective-permute-start.5
  277.3 45.6 %collective-permute-done.4 = f32[3,256,768]{2,1,0:T(8,128)S(1)} collective-permute-done((f32[3,256,768]{2,1,0:T(8,128)S(1)}, f32[3,256,768]{2,1,0:T(8,128)S(1)}, u32[]{:S(2)}, u32[]{:S(2)}) %collective-permute-start.4) | collective-permute-done | bytes 2359328 | tf_op jit(solution)/shard_map/ppermute | solution.py:25
  323.0 22.8 %collective-permute-done.5 = f32[3,256,768]{2,1,0:T(8,128)S(1)} collective-permute-done((f32[3,256,768]{2,1,0:T(8,128)S(1)}, f32[3,256,768]{2,1,0:T(8,128)S(1)}, u32[]{:S(2)}, u32[]{:S(2)}) %collective-permute-start.5) | collective-permute-done | bytes 2359328 | tf_op jit(solution)/shard_map/ppermute | solution.py:25
  347.2 1.9 collective-permute-start.7
  349.9 5.7 %collective-permute-start.6 = (bf16[1,256,768]{2,1,0:T(8,128)(2,1)}, bf16[1,256,768]{2,1,0:T(8,128)(2,1)}, u32[]{:S(2)}, u32[]{:S(2)}) collective-permute-start(bf16[1,256,768]{2,1,0:T(8,128)(2,1)} %fusion.72), channel_id=1, source_target_pairs={{64,0},{128,64},{192,128},{65,1},{129,65},{193,129},{66,2},{130,66... | collective-permute-start | bytes 1179656 | tf_op jit(solution)/shard_map/ppermute | solution.py:25
  356.5 1.8 reduce.39
  359.1 4.4 %all-to-all-start.6 = ((bf16[8,2,6144]{2,1,0:T(2,128)(2,1)}), bf16[8,2,6144]{2,1,0:T(2,128)(2,1)S(1)}, u32[]{:S(2)}, u32[]{:S(2)}) async-start(bf16[8,2,6144]{2,1,0:T(2,128)(2,1)} %reshape.1193), calls=%async_computation.6 | async-start | bytes 393216 | tf_op jit(solution)/shard_map/all_to_all | solution.py:119
  363.5 3.7 collective-permute-done.7
  367.2 1.4 fusion.64
  368.9 1.8 reduce.41
  371.4 4.4 %all-to-all-start.8 = ((bf16[8,2,6144]{2,1,0:T(2,128)(2,1)}), bf16[8,2,6144]{2,1,0:T(2,128)(2,1)S(1)}, u32[]{:S(2)}, u32[]{:S(2)}) async-start(bf16[8,2,6144]{2,1,0:T(2,128)(2,1)} %reshape.1197), calls=%async_computation.8 | async-start | bytes 393216 | tf_op jit(solution)/shard_map/all_to_all | solution.py:121
  376.1 1.8 reduce.40
  378.6 4.0 %all-to-all-done.8 = bf16[8,2,6144]{2,1,0:T(2,128)(2,1)S(1)} async-done(((bf16[8,2,6144]{2,1,0:T(2,128)(2,1)}), bf16[8,2,6144]{2,1,0:T(2,128)(2,1)S(1)}, u32[]{:S(2)}, u32[]{:S(2)}) %all-to-all-start.8) | async-done | bytes 196640 | tf_op jit(solution)/shard_map/all_to_all | solution.py:121
  382.6 3.4 all-to-all-start.7
  387.9 4.9 %all-to-all-done.7 = bf16[8,2,6144]{2,1,0:T(2,128)(2,1)S(1)} async-done(((bf16[8,2,6144]{2,1,0:T(2,128)(2,1)}), bf16[8,2,6144]{2,1,0:T(2,128)(2,1)S(1)}, u32[]{:S(2)}, u32[]{:S(2)}) %all-to-all-start.7) | async-done | bytes 196640 | tf_op jit(solution)/shard_map/all_to_all | solution.py:120
  (243 shorter events, 57.6 us)
Async XLA Ops:
  0.6 26.7 %all-to-all-start.3 = ((f32[1,1,32,24]{2,1,0,3:T(1,128)}), f32[1,1,32,24]{2,1,0,3:T(1,128)S(1)}, u32[]{:S(2)}, u32[]{:S(2)}) async-start(f32[1,1,32,24]{2,1,0,3:T(1,128)} %bitcast.446), calls=%async_computation.3 | async-start | bytes 24576 | tf_op jit(solution)/shard_map/all_to_all | solution.py:65
  5.1 27.2 %copy-start.45 = (bf16[1,1,32,3072]{3,2,1,0:T(8,128)(2,1)S(1)}, bf16[1,1,32,3072]{3,2,1,0:T(8,128)(2,1)}, u32[]{:S(2)}) copy-start(bf16[1,1,32,3072]{3,2,1,0:T(8,128)(2,1)} %param.34) | copy-start | bytes 589828
  27.3 25.2 %all-to-all-start = ((bf16[8,2,6144]{2,1,0:T(2,128)(2,1)}), bf16[8,2,6144]{2,1,0:T(2,128)(2,1)S(1)}, u32[]{:S(2)}, u32[]{:S(2)}) async-start(bf16[8,2,6144]{2,1,0:T(2,128)(2,1)} %reshape.1185), calls=%async_computation | async-start | bytes 393216 | tf_op jit(solution)/shard_map/all_to_all | solution.py:60
  32.4 25.3 %copy-start.46 = (bf16[1,1,32,3072]{3,2,1,0:T(8,128)(2,1)S(1)}, bf16[1,1,32,3072]{3,2,1,0:T(8,128)(2,1)}, u32[]{:S(2)}) copy-start(bf16[1,1,32,3072]{3,2,1,0:T(8,128)(2,1)} %param.32) | copy-start | bytes 589828
  52.6 25.3 %all-to-all-start.1 = ((bf16[8,2,6144]{2,1,0:T(2,128)(2,1)}), bf16[8,2,6144]{2,1,0:T(2,128)(2,1)S(1)}, u32[]{:S(2)}, u32[]{:S(2)}) async-start(bf16[8,2,6144]{2,1,0:T(2,128)(2,1)} %reshape.1183), calls=%async_computation.1 | async-start | bytes 393216 | tf_op jit(solution)/shard_map/all_to_all | solution.py:61
  57.7 25.4 %copy-start.47 = (bf16[1,1,32,3072]{3,2,1,0:T(8,128)(2,1)S(1)}, bf16[1,1,32,3072]{3,2,1,0:T(8,128)(2,1)}, u32[]{:S(2)}) copy-start(bf16[1,1,32,3072]{3,2,1,0:T(8,128)(2,1)} %param.36) | copy-start | bytes 589828
  77.9 57.6 %all-to-all-start.2 = ((bf16[8,2,6144]{2,1,0:T(2,128)(2,1)}), bf16[8,2,6144]{2,1,0:T(2,128)(2,1)S(1)}, u32[]{:S(2)}, u32[]{:S(2)}) async-start(bf16[8,2,6144]{2,1,0:T(2,128)(2,1)} %reshape.1187), calls=%async_computation.2 | async-start | bytes 393216 | tf_op jit(solution)/shard_map/all_to_all | solution.py:59
  83.1 20.2 %copy-start.48 = (bf16[1,1,32,3072]{3,2,1,0:T(8,128)(2,1)S(1)}, bf16[1,1,32,3072]{3,2,1,0:T(8,128)(2,1)}, u32[]{:S(2)}) copy-start(bf16[1,1,32,3072]{3,2,1,0:T(8,128)(2,1)} %param.35) | copy-start | bytes 589828
  103.3 37.6 %copy-start.49 = (s32[4]{0:T(128)S(1)}, s32[4]{0:T(128)}, u32[]{:S(2)}) copy-start(s32[4]{0:T(128)} %constant.394.clone.1) | copy-start | bytes 52
  135.5 18.7 %copy-start.37 = (bf16[8,2,6144]{2,1,0:T(2,128)(2,1)}, bf16[8,2,6144]{2,1,0:T(2,128)(2,1)S(1)}, u32[]{:S(2)}) copy-start(bf16[8,2,6144]{2,1,0:T(2,128)(2,1)S(1)} %all-to-all-done.2) | copy-start | bytes 589828
  135.5 11.6 %all-to-all-start.4 = ((bf16[8,2,6144]{2,1,0:T(2,128)(2,1)}), bf16[8,2,6144]{2,1,0:T(2,128)(2,1)S(1)}, u32[]{:S(2)}, u32[]{:S(2)}) async-start(bf16[8,2,6144]{2,1,0:T(2,128)(2,1)} %reshape.1189), calls=%async_computation.4 | async-start | bytes 393216 | tf_op jit(solution)/shard_map/all_to_all | solution.py:63
  147.1 4.7 %copy-start.39 = (bf16[8,2,6144]{2,1,0:T(2,128)(2,1)}, bf16[8,2,6144]{2,1,0:T(2,128)(2,1)S(1)}, u32[]{:S(2)}) copy-start(bf16[8,2,6144]{2,1,0:T(2,128)(2,1)S(1)} %all-to-all-done.4) | copy-start | bytes 589828
  147.1 24.3 %all-to-all-start.5 = ((bf16[8,2,6144]{2,1,0:T(2,128)(2,1)}), bf16[8,2,6144]{2,1,0:T(2,128)(2,1)}, u32[]{:S(2)}, u32[]{:S(2)}) async-start(bf16[8,2,6144]{2,1,0:T(2,128)(2,1)} %reshape.1191), calls=%async_computation.5 | async-start | bytes 393216 | tf_op jit(solution)/shard_map/all_to_all | solution.py:62
  155.1 11.2 %copy-start.38 = (bf16[8,2,6144]{2,1,0:T(2,128)(2,1)S(1)}, bf16[8,2,6144]{2,1,0:T(2,128)(2,1)}, u32[]{:S(2)}) copy-start(bf16[8,2,6144]{2,1,0:T(2,128)(2,1)} %copy-done.37) | copy-start | bytes 589828
  157.4 22.5 %collective-permute-start = (bf16[1,1,256,768]{3,2,1,0:T(8,128)(2,1)}, bf16[1,1,256,768]{3,2,1,0:T(8,128)(2,1)S(1)}, u32[]{:S(2)}, u32[]{:S(2)}) collective-permute-start(bf16[1,1,256,768]{3,2,1,0:T(8,128)(2,1)} %pad_maximum_fusion.1), channel_id=1, source_target_pairs={{0,64},{64,128},{128,192},{1,65},{65,129},{129,193},{2,66},{66,130... | collective-permute-start | bytes 1179656 | tf_op jit(solution)/shard_map/ppermute | solution.py:14
  162.9 23.3 %collective-permute-start.1 = (bf16[1,1,256,768]{3,2,1,0:T(8,128)(2,1)}, bf16[1,1,256,768]{3,2,1,0:T(8,128)(2,1)S(1)}, u32[]{:S(2)}, u32[]{:S(2)}) collective-permute-start(bf16[1,1,256,768]{3,2,1,0:T(8,128)(2,1)} %pad_maximum_fusion.1), channel_id=1, source_target_pairs={{64,0},{128,64},{192,128},{65,1},{129,65},{193,129},{66,2},{130,66... | collective-permute-start | bytes 1179656 | tf_op jit(solution)/shard_map/ppermute | solution.py:17
  166.3 2.6 copy-start.40
  175.1 1.0 copy-start.35
  175.2 1.4 copy-start.36
  176.3 2.1 copy-start.6
  187.3 31.4 %collective-permute-start.2 = (bf16[3,1,256,768]{3,2,1,0:T(8,128)(2,1)}, bf16[3,1,256,768]{3,2,1,0:T(8,128)(2,1)}, u32[]{:S(2)}, u32[]{:S(2)}) collective-permute-start(bf16[3,1,256,768]{3,2,1,0:T(8,128)(2,1)} %pad_maximum_fusion), channel_id=1, source_target_pairs={{0,8},{8,16},{16,24},{24,32},{32,40},{40,48},{48,56},{1,9},{9,17},... | collective-permute-start | bytes 3538952 | tf_op jit(solution)/shard_map/ppermute | solution.py:14
  190.7 33.9 %collective-permute-start.3 = (bf16[3,1,256,768]{3,2,1,0:T(8,128)(2,1)}, bf16[3,1,256,768]{3,2,1,0:T(8,128)(2,1)}, u32[]{:S(2)}, u32[]{:S(2)}) collective-permute-start(bf16[3,1,256,768]{3,2,1,0:T(8,128)(2,1)} %pad_maximum_fusion), channel_id=1, source_target_pairs={{8,0},{16,8},{24,16},{32,24},{40,32},{48,40},{56,48},{9,1},{17,9},... | collective-permute-start | bytes 3538952 | tf_op jit(solution)/shard_map/ppermute | solution.py:17
  195.5 1.4 copy-start.8
  198.9 2.1 copy-start.10
  227.0 1.4 copy-start.12
  235.7 2.5 copy-start.4
  237.5 0.9 copy-start.43
  243.7 5.4 %copy-start.18 = (bf16[1,1,256,384]{2,3,1,0:T(8,128)(2,1)}, bf16[1,1,256,384]{2,3,1,0:T(8,128)(2,1)S(1)}, u32[]{:S(2)}) copy-start(bf16[1,1,256,384]{2,3,1,0:T(8,128)(2,1)S(1)} %copy.644) | copy-start | bytes 589828
  245.5 1.4 copy-start.44
  246.9 7.1 %copy-start.41 = (bf16[1,1,256,384]{3,2,1,0:T(8,128)(2,1)S(1)}, bf16[1,1,256,384]{3,2,1,0:T(8,128)(2,1)}, u32[]{:S(2)}) copy-start(bf16[1,1,256,384]{3,2,1,0:T(8,128)(2,1)} %get-tuple-element.162) | copy-start | bytes 589828
  254.0 2.3 copy-start.16
  254.8 1.4 copy-start.42
  260.7 1.9 copy-start.33
  260.7 1.9 copy-start.34
  262.6 1.6 copy-start.24
  262.6 1.6 copy-start.25
  262.6 3.6 copy-start.26
  262.6 3.6 copy-start.27
  264.2 2.3 copy-start.20
  264.2 2.3 copy-start.21
  266.2 1.0 copy-start.28
  266.2 1.1 copy-start.29
  266.4 1.1 copy-start.30
  266.4 1.2 copy-start.31
  267.3 1.1 copy-start.22
  267.3 1.2 copy-start.23
  267.6 1.1 copy-start.32
  268.8 6.7 %copy-start.7 = (bf16[256,3,128]{0,2,1:T(8,128)(2,1)S(1)}, bf16[256,3,128]{0,2,1:T(8,128)(2,1)}, u32[]{:S(2)}) copy-start(bf16[256,3,128]{0,2,1:T(8,128)(2,1)} %copy-done.6) | copy-start | bytes 589828
  268.9 7.0 %copy-start.9 = (bf16[1,1,256,384]{2,3,1,0:T(8,128)(2,1)S(1)}, bf16[1,1,256,384]{2,3,1,0:T(8,128)(2,1)}, u32[]{:S(2)}) copy-start(bf16[1,1,256,384]{2,3,1,0:T(8,128)(2,1)} %copy-done.8) | copy-start | bytes 589828
  268.9 7.3 %copy-start.11 = (bf16[1,1,256,384]{2,3,1,0:T(8,128)(2,1)S(1)}, bf16[1,1,256,384]{2,3,1,0:T(8,128)(2,1)}, u32[]{:S(2)}) copy-start(bf16[1,1,256,384]{2,3,1,0:T(8,128)(2,1)} %copy-done.10) | copy-start | bytes 589828
  269.4 6.9 %copy-start.13 = (bf16[1,1,256,384]{2,3,1,0:T(8,128)(2,1)S(1)}, bf16[1,1,256,384]{2,3,1,0:T(8,128)(2,1)}, u32[]{:S(2)}) copy-start(bf16[1,1,256,384]{2,3,1,0:T(8,128)(2,1)} %copy-done.12) | copy-start | bytes 589828
  269.4 7.1 %copy-start.15 = (bf16[1,1,256,384]{2,3,1,0:T(8,128)(2,1)S(1)}, bf16[1,1,256,384]{2,3,1,0:T(8,128)(2,1)}, u32[]{:S(2)}) copy-start(bf16[1,1,256,384]{2,3,1,0:T(8,128)(2,1)} %copy-done.14) | copy-start | bytes 589828
  269.5 53.5 %collective-permute-start.4 = (f32[3,256,768]{2,1,0:T(8,128)S(1)}, f32[3,256,768]{2,1,0:T(8,128)S(1)}, u32[]{:S(2)}, u32[]{:S(2)}) collective-permute-start(f32[3,256,768]{2,1,0:T(8,128)S(1)} %get-tuple-element.159), channel_id=1, source_target_pairs={{8,0},{16,8},{24,16},{32,24},{40,32},{48,40},{56,48},{9,1},{17,9},... | collective-permute-start | bytes 7077896 | tf_op jit(solution)/shard_map/ppermute | solution.py:25
  273.2 3.6 copy-start.1
  273.2 3.6 copy-start.19
  273.2 72.5 %collective-permute-start.5 = (f32[3,256,768]{2,1,0:T(8,128)S(1)}, f32[3,256,768]{2,1,0:T(8,128)S(1)}, u32[]{:S(2)}, u32[]{:S(2)}) collective-permute-start(f32[3,256,768]{2,1,0:T(8,128)S(1)} %get-tuple-element.160), channel_id=1, source_target_pairs={{0,8},{8,16},{16,24},{24,32},{32,40},{40,48},{48,56},{1,9},{9,17},... | collective-permute-start | bytes 7077896 | tf_op jit(solution)/shard_map/ppermute | solution.py:25
  275.9 1.2 copy-start.3
  346.2 9.4 %copy-start.17 = (bf16[1,1,256,384]{2,3,1,0:T(8,128)(2,1)S(1)}, bf16[1,1,256,384]{2,3,1,0:T(8,128)(2,1)}, u32[]{:S(2)}) copy-start(bf16[1,1,256,384]{2,3,1,0:T(8,128)(2,1)} %copy-done.16) | copy-start | bytes 589828
  346.2 9.6 %copy-start.5 = (bf16[1,1,256,384]{2,3,1,0:T(8,128)(2,1)S(1)}, bf16[1,1,256,384]{2,3,1,0:T(8,128)(2,1)}, u32[]{:S(2)}) copy-start(bf16[1,1,256,384]{2,3,1,0:T(8,128)(2,1)} %copy-done.4) | copy-start | bytes 589828
  347.2 20.0 %collective-permute-start.7 = (f32[1,256,768]{2,1,0:T(8,128)}, f32[1,256,768]{2,1,0:T(8,128)}, u32[]{:S(2)}, u32[]{:S(2)}) collective-permute-start(f32[1,256,768]{2,1,0:T(8,128)} %slice_bitcast_fusion.2), channel_id=1, source_target_pairs={{0,64},{64,128},{128,192},{1,65},{65,129},{129,193},{2,66},{66,130... | collective-permute-start | bytes 2359304 | tf_op jit(solution)/shard_map/ppermute | solution.py:25
  349.9 13.6 %collective-permute-start.6 = (bf16[1,256,768]{2,1,0:T(8,128)(2,1)}, bf16[1,256,768]{2,1,0:T(8,128)(2,1)}, u32[]{:S(2)}, u32[]{:S(2)}) collective-permute-start(bf16[1,256,768]{2,1,0:T(8,128)(2,1)} %fusion.72), channel_id=1, source_target_pairs={{64,0},{128,64},{192,128},{65,1},{129,65},{193,129},{66,2},{130,66... | collective-permute-start | bytes 1179656 | tf_op jit(solution)/shard_map/ppermute | solution.py:25
  359.1 12.3 %all-to-all-start.6 = ((bf16[8,2,6144]{2,1,0:T(2,128)(2,1)}), bf16[8,2,6144]{2,1,0:T(2,128)(2,1)S(1)}, u32[]{:S(2)}, u32[]{:S(2)}) async-start(bf16[8,2,6144]{2,1,0:T(2,128)(2,1)} %reshape.1193), calls=%async_computation.6 | async-start | bytes 393216 | tf_op jit(solution)/shard_map/all_to_all | solution.py:119
  371.4 11.2 %all-to-all-start.8 = ((bf16[8,2,6144]{2,1,0:T(2,128)(2,1)}), bf16[8,2,6144]{2,1,0:T(2,128)(2,1)S(1)}, u32[]{:S(2)}, u32[]{:S(2)}) async-start(bf16[8,2,6144]{2,1,0:T(2,128)(2,1)} %reshape.1197), calls=%async_computation.8 | async-start | bytes 393216 | tf_op jit(solution)/shard_map/all_to_all | solution.py:121
  382.6 10.2 %all-to-all-start.7 = ((bf16[8,2,6144]{2,1,0:T(2,128)(2,1)}), bf16[8,2,6144]{2,1,0:T(2,128)(2,1)S(1)}, u32[]{:S(2)}, u32[]{:S(2)}) async-start(bf16[8,2,6144]{2,1,0:T(2,128)(2,1)} %reshape.1195), calls=%async_computation.7 | async-start | bytes 393216 | tf_op jit(solution)/shard_map/all_to_all | solution.py:120
  (3 other events, 2.3 us)
where the time goes:
time: 401 us; the launch traced here: 394 us
  other arithmetic  113 us (28%)
  waiting for transfers between devices  110 us (27%)
  local copies, waits for them, and re-layouts  81.7 us (20%)
  starting transfers between devices  69.7 us (17%)
  matrix products  16.8 us (4%)
    unnamed x8, other arithmetic  102 us
    ppermute x4, waiting for transfers between devices, passed_along(): return lax.ppermute(array, axis, pairs)  72.1 us
    unnamed x131, local copies, waits for them, and re-layouts  30 us
    ppermute x2, waiting for transfers between devices, padded(): lax.ppermute(lax.slice_in_dim(block, block.shape[dim] - width, None, axis...  17.1 us
    ppermute x4, starting transfers between devices, passed_along(): return lax.ppermute(array, axis, pairs)  13.7 us
    reshape x9, local copies, waits for them, and re-layouts, per_device(): key_part.reshape(rows_h, rows_w, tile_len, chan_loc)  10.6 us
    reshape x9, local copies, waits for them, and re-layouts, per_device(): value_part.reshape(rows_h, rows_w, tile_len, chan_loc)  10.3 us
    slice x12, local copies, waits for them, and re-layouts, per_device(): value_tiles = split_heads(window[..., chan_loc:], heads_loc)  9.8 us
  transfers between devices with their start and end apart: 17, of which 9 were waited for; matrix products, arithmetic and copies ran while one was open for 42% of the time, Pallas kernels for 0%

commit v1 on v0

v1 whole, which is shorter than its diff:
```python
import jax
import jax.numpy as jnp
from jax import lax
from jax.experimental import pallas as pl
from jax.experimental.pallas import tpu as pltpu
from jax.sharding import PartitionSpec as P

HD = 128
MESH = pl.DeviceIdType.MESH
F32 = jnp.float32
BF16 = jnp.bfloat16
NT = (((1,), (1,)), ((), ()))
NN = (((1,), (0,)), ((), ()))


def dot(a, b, dims):
    return lax.dot_general(a, b, dims, preferred_element_type=F32)


def body(
    nh, nw, nd, heads, tok,
    q_hbm, k_hbm, v_hbm, o_hbm, g_hbm, n_hbm,
    res,
    xin, o_in, n_in, qd, kv, pad, st_out, st_in, st,
    k_t, dq_acc, kv_acc, rq_send, rq_recv, rk_send, rk_recv, out_send,
    sem_load, s_in, r_in, s_st, r_st, s_z, r_z, s_x, r_x, s_sz, r_sz,
    s_rq, r_rq, s_rk, r_rk, s_out, r_out,
):
    ih, iw, me = lax.axis_index("ha"), lax.axis_index("wa"), lax.axis_index("hd")
    tile = nd * tok
    scale = HD ** -0.5
    sides_h = (("ha", ih > 0, ih - 1, 0, 2), ("ha", ih < nh - 1, ih + 1, 2, 0))
    sides_w = (("wa", iw > 0, iw - 1, 0, 2), ("wa", iw < nw - 1, iw + 1, 2, 0))

    barrier = pltpu.get_barrier_semaphore()

    def greet(t, c):
        pl.semaphore_signal(barrier, inc=1, device_id={"hd": lax.rem(me + 1 + t, nd)}, device_id_type=MESH)
        return c

    lax.fori_loop(0, nd - 1, greet, 0)
    for axis, exists, other, _, _ in sides_h + sides_w:
        @pl.when(exists)
        def _():
            pl.semaphore_signal(barrier, inc=1, device_id={axis: other}, device_id_type=MESH)

    loads = [
        pltpu.make_async_copy(src, dst, sem_load.at[n])
        for n, (src, dst) in enumerate((
            (q_hbm, xin.at[0]), (g_hbm, xin.at[1]), (k_hbm, xin.at[2]), (v_hbm, xin.at[3]),
            (o_hbm, o_in), (n_hbm, n_in),
        ))
    ]
    for load in loads:
        load.start()

    for _, exists, _, slot, _ in sides_h:
        @pl.when(jnp.logical_not(exists))
        def _():
            qd[slot] = jnp.zeros(qd.shape[1:], BF16)
            st[slot] = jnp.zeros(st.shape[1:], F32)
            rq_recv[slot // 2] = jnp.zeros(rq_recv.shape[1:], BF16)
    for _, exists, _, slot, _ in sides_w:
        @pl.when(jnp.logical_not(exists))
        def _():
            kv[slot] = jnp.zeros(kv.shape[1:], BF16)
            rk_recv[slot // 2] = jnp.zeros(rk_recv.shape[1:], BF16)

    for load in loads[:4]:
        load.wait()
    count = jnp.int32(nd - 1)
    for _, exists, _, _, _ in sides_h + sides_w:
        count = count + exists.astype(jnp.int32)
    pl.semaphore_wait(barrier, count)

    my_rows = pl.ds(pl.multiple_of(me * tok, tok), tok)

    def spread(h, part, dst):
        def lanes(d):
            return pl.ds(pl.multiple_of(d * (heads * HD) + h * HD, HD), HD)

        def one(t, c):
            d = lax.rem(me + 1 + t, nd)
            pltpu.make_async_remote_copy(
                src_ref=xin.at[pl.ds(2 * part, 2), :, lanes(d)],
                dst_ref=dst.at[1, h, :, my_rows, :],
                send_sem=s_in.at[h, part, t], recv_sem=r_in.at[h, part],
                device_id={"hd": d}, device_id_type=MESH,
            ).start()
            return c

        lax.fori_loop(0, nd - 1, one, 0)
        pltpu.make_async_copy(
            xin.at[pl.ds(2 * part, 2), :, lanes(me)], dst.at[1, h, :, my_rows, :], r_in.at[h, part]
        ).start()

    for h in range(heads):
        spread(h, 0, qd)
        spread(h, 1, kv)

    for load in loads[4:]:
        load.wait()
    lane = lax.broadcasted_iota(jnp.int32, (tok, 128), 1)
    table = jnp.zeros((tok, 128), F32)
    norms = n_in[...]
    for g in range(nd * heads):
        d, h = g // heads, g % heads
        cols = slice(g * HD, (g + 1) * HD)
        dots = jnp.sum(xin[1, :, cols].astype(F32) * o_in[:, cols].astype(F32), axis=1, keepdims=True)
        table = jnp.where(lane == 8 * d + h, norms[:, g:g + 1], table)
        table = jnp.where(lane == 8 * d + heads + h, dots, table)
    pad[...] = jnp.zeros(pad.shape, F32)
    pad[pl.ds(pl.multiple_of(lax.rem(me, 4) * tok, tok), tok), :] = table
    st_out[...] = pad[...].T

    def spread_stats(t, c):
        d = lax.rem(me + 1 + t, nd)
        pltpu.make_async_remote_copy(
            src_ref=st_out.at[pl.ds(pl.multiple_of(d * 8, 8), 8), :], dst_ref=st_in.at[me],
            send_sem=s_st.at[t], recv_sem=r_st.at[0], device_id={"hd": d}, device_id_type=MESH,
        ).start()
        return c

    lax.fori_loop(0, nd - 1, spread_stats, 0)
    pltpu.make_async_copy(
        st_out.at[pl.ds(pl.multiple_of(me * 8, 8), 8), :], st_in.at[me], r_st.at[0]
    ).start()

    def halo(buf, h, side, send, recv):
        axis, _, other, slot, there = side
        return pltpu.make_async_remote_copy(
            src_ref=buf.at[1, h], dst_ref=buf.at[there, h],
            send_sem=send.at[h, slot // 2], recv_sem=recv.at[h, there // 2],
            device_id={axis: other}, device_id_type=MESH,
        )

    def halo_stats(side):
        axis, _, other, slot, there = side
        return pltpu.make_async_remote_copy(
            src_ref=st.at[1], dst_ref=st.at[there],
            send_sem=s_sz.at[slot // 2], recv_sem=r_sz.at[there // 2],
            device_id={axis: other}, device_id_type=MESH,
        )

    def when(side, fn):
        @pl.when(side[1])
        def _():
            fn()

    for h in range(heads):
        pltpu.make_async_copy(qd.at[1, h], qd.at[1, h], r_in.at[h, 0]).wait()
        for side in sides_h:
            when(side, lambda: halo(qd, h, side, s_z, r_z).start())
        pltpu.make_async_copy(kv.at[1, h], kv.at[1, h], r_in.at[h, 1]).wait()
        for side in sides_w:
            when(side, lambda: halo(kv, h, side, s_x, r_x).start())
        if h == 0:
            pltpu.make_async_copy(st_in, st_in, r_st.at[0]).wait()
            got = st_in[...]
            st[1] = jnp.concatenate(
                [got[0] + got[1] + got[2] + got[3], got[4] + got[5] + got[6] + got[7]], axis=1
            )
            for side in sides_h:
                when(side, lambda: halo_stats(side).start())

    def arrived(buf, slot, h, sem):
        pltpu.make_async_copy(buf.at[slot, h], buf.at[slot, h], sem.at[h, slot // 2]).wait()

    def back_q(h, side):
        axis, _, other, slot, there = side
        return pltpu.make_async_remote_copy(
            src_ref=rq_send.at[slot // 2, h], dst_ref=rq_recv.at[there // 2, h],
            send_sem=s_rq.at[slot // 2, h], recv_sem=r_rq.at[there // 2, h],
            device_id={axis: other}, device_id_type=MESH,
        )

    def back_kv(h, side):
        axis, _, other, slot, there = side
        return pltpu.make_async_remote_copy(
            src_ref=rk_send.at[slot // 2, h], dst_ref=rk_recv.at[there // 2, h],
            send_sem=s_rk.at[slot // 2, h], recv_sem=r_rk.at[there // 2, h],
            device_id={axis: other}, device_id_type=MESH,
        )

    def out_copy(h, t):
        d = lax.rem(me + 1 + t, nd)
        return pltpu.make_async_remote_copy(
            src_ref=out_send.at[h, :, pl.ds(pl.multiple_of(d * tok, tok), tok), :],
            dst_ref=res.at[:, :, pl.ds(pl.multiple_of(me * (heads * HD) + h * HD, HD), HD)],
            send_sem=s_out.at[h, t], recv_sem=r_out.at[h],
            device_id={"hd": d}, device_id_type=MESH,
        )

    def compute(h):
        for side in sides_w:
            when(side, lambda: arrived(kv, side[3], h, r_x))
        for b in range(3):
            k_t[b] = kv[b, h, 0].T
        for n, a in enumerate((1, 0, 2)):
            if a != 1:
                side = sides_h[a // 2]
                when(side, lambda: arrived(qd, a, h, r_z))

                @pl.when(side[1] & (h == 0))
                def _():
                    pltpu.make_async_copy(st.at[a], st.at[a], r_sz.at[a // 2]).wait()
            q, g = qd[a, h, 0], qd[a, h, 1]
            norm = st[a, pl.ds(h, 1), :]
            dots = st[a, pl.ds(heads + h, 1), :]
            dq = None
            for b in range(3):
                s_t = dot(kv[b, h, 0], q, NT)
                p_t = jnp.exp(s_t * scale - norm)
                dp_t = dot(kv[b, h, 1], g, NT)
                ds_t = (p_t * (dp_t - dots) * scale).astype(BF16)
                dk = dot(ds_t, q, NN)
                dv = dot(p_t.astype(BF16), g, NN)
                term = dot(k_t[b], ds_t, NN)
                dq = term if dq is None else dq + term
                if n == 0:
                    kv_acc[h, b, 0] = dk
                    kv_acc[h, b, 1] = dv
                else:
                    kv_acc[h, b, 0] += dk
                    kv_acc[h, b, 1] += dv
            if a == 1:
                dq_acc[h] = dq
            else:
                rq_send[a // 2, h] = dq.astype(BF16)
                when(sides_h[a // 2], lambda: back_q(h, sides_h[a // 2]).start())
        for side in sides_w:
            slot = side[3]
            rk_send[slot // 2, h] = kv_acc[h, slot].astype(BF16)
            when(side, lambda: back_kv(h, side).start())

    def finish(h):
        for n, side in enumerate(sides_h):
            when(side, lambda: pltpu.make_async_copy(
                rq_recv.at[n, h], rq_recv.at[n, h], r_rq.at[n, h]).wait())
        for n, side in enumerate(sides_w):
            when(side, lambda: pltpu.make_async_copy(
                rk_recv.at[n, h], rk_recv.at[n, h], r_rk.at[n, h]).wait())
        dq = dq_acc[h] + rq_recv[0, h].astype(F32) + rq_recv[1, h].astype(F32)
        out_send[h, 0] = dq.T.astype(BF16)
        for n in range(2):
            out_send[h, 1 + n] = (
                kv_acc[h, 1, n] + rk_recv[0, h, n].astype(F32) + rk_recv[1, h, n].astype(F32)
            ).astype(BF16)

        def one(t, c):
            out_copy(h, t).start()
            return c

        lax.fori_loop(0, nd - 1, one, 0)
        pltpu.make_async_copy(
            out_send.at[h, :, my_rows, :],
            res.at[:, :, pl.ds(pl.multiple_of(me * (heads * HD) + h * HD, HD), HD)],
            r_out.at[h],
        ).start()

    def step(h, c):
        compute(h)

        @pl.when(h > 0)
        def _():
            finish(h - 1)
        return c

    lax.fori_loop(0, heads, step, 0)
    finish(heads - 1)

    def drain(t, c):
        d = lax.rem(me + 1 + t, nd)
        for h in range(heads):
            for part in range(2):
                src = xin.at[pl.ds(2 * part, 2), :, pl.ds(0, HD)]
                pltpu.make_async_copy(src, src, s_in.at[h, part, t]).wait()
            src = out_send.at[h, :, pl.ds(0, tok), :]
            pltpu.make_async_copy(src, src, s_out.at[h, t]).wait()
        src = st_out.at[pl.ds(0, 8), :]
        pltpu.make_async_copy(src, src, s_st.at[t]).wait()
        return c

    lax.fori_loop(0, nd - 1, drain, 0)
    for side in sides_h:
        when(side, lambda: halo_stats(side).wait_send())
    for h in range(heads):
        for side in sides_h:
            when(side, lambda: halo(qd, h, side, s_z, r_z).wait_send())
            when(side, lambda: back_q(h, side).wait_send())
        for side in sides_w:
            when(side, lambda: halo(kv, h, side, s_x, r_x).wait_send())
            when(side, lambda: back_kv(h, side).wait_send())
    for h in range(heads):
        part = res.at[:, :, pl.ds(0, nd * HD)]
        pltpu.make_async_copy(part, part, r_out.at[h]).wait()


def solution(mesh):
    nh, nw, nd = mesh.shape["ha"], mesh.shape["wa"], mesh.shape["hd"]
    spec = P("ha", "wa", "hd", None)

    def per_device(q, k, v, o, g, n):
        tok, chan = q.shape[2], q.shape[3]
        heads = chan // HD // nd
        tile = tok * nd
        lead = q.shape

        def kernel(*refs):
            body(nh, nw, nd, heads, tok, *refs)

        dma = pltpu.SemaphoreType.DMA
        res = pl.pallas_call(
            kernel,
            out_shape=jax.ShapeDtypeStruct((3, tok, chan), BF16),
            in_specs=[pl.BlockSpec(memory_space=pl.ANY)] * 6,
            out_specs=pl.BlockSpec(memory_space=pltpu.VMEM),
            scratch_shapes=[
                pltpu.VMEM((4, tok, chan), BF16),
                pltpu.VMEM((tok, chan), BF16),
                pltpu.VMEM((tok, n.shape[3]), F32),
                pltpu.VMEM((3, heads, 2, tile, HD), BF16),
                pltpu.VMEM((3, heads, 2, tile, HD), BF16),
                pltpu.VMEM((128, 128), F32),
                pltpu.VMEM((128, 128), F32),
                pltpu.VMEM((nd, 8, 128), F32),
                pltpu.VMEM((3, 8, tile), F32),
                pltpu.VMEM((3, HD, tile), BF16),
                pltpu.VMEM((heads, HD, tile), F32),
                pltpu.VMEM((heads, 3, 2, tile, HD), F32),
                pltpu.VMEM((2, heads, HD, tile), BF16),
                pltpu.VMEM((2, heads, HD, tile), BF16),
                pltpu.VMEM((2, heads, 2, tile, HD), BF16),
                pltpu.VMEM((2, heads, 2, tile, HD), BF16),
                pltpu.VMEM((heads, 3, tile, HD), BF16),
                dma((6,)),
                dma((heads, 2, nd - 1)), dma((heads, 2)),
                dma((nd - 1,)), dma((1,)),
                dma((heads, 2)), dma((heads, 2)),
                dma((heads, 2)), dma((heads, 2)),
                dma((2,)), dma((2,)),
                dma((2, heads)), dma((2, heads)),
                dma((2, heads)), dma((2, heads)),
                dma((heads, nd - 1)), dma((heads,)),
            ],
            compiler_params=pltpu.CompilerParams(
                collective_id=0, has_side_effects=True, vmem_limit_bytes=48 * 1024 * 1024
            ),
        )(*(x.reshape(x.shape[2:]) for x in (q, k, v, o, g, n)))
        return tuple(res[i].reshape(lead) for i in range(3))

    return jax.shard_map(
        per_device, mesh=mesh, in_specs=(spec,) * 6, out_specs=(spec,) * 3, check_vma=False
    )
```

time: 401 us -> 69.5 us (0.17)
  the two profiles are of different devices: /device:TPU:96 before, /device:TPU:71 now
where the time goes in v1:
time: 69.5 us; the launch traced here: 69.2 us
  Pallas kernels  62.3 us (90%)
  local copies, waits for them, and re-layouts  6.23 us (9%)
    pallas_call x1, Pallas kernels, per_device(): pl.pallas_call(kernel, out_shape=jax.ShapeDtypeStruct((3, tok, chan), BF1...  62.3 us
    unnamed x11, local copies, waits for them, and re-layouts  5.41 us

profile of v1, /device:TPU:71, one launch (start us, length us, event | category | flops | bytes accessed | tf_op | source)
XLA Modules:
  0.0 69.2 jit_solution(6109466379175700452)
XLA Ops:
  0.6 0.8 %copy.9 = f32[1,1,32,24]{3,2,1,0:T(8,128)S(1)} copy(f32[1,1,32,24]{2,3,1,0:T(8,128)} %param.11) | data formatting | bytes 6144 | tf_op args[5]
  1.4 0.0 copy-start
  1.4 0.9 %copy-done = bf16[1,1,32,3072]{3,2,1,0:T(8,128)(2,1)S(1)} copy-done((bf16[1,1,32,3072]{3,2,1,0:T(8,128)(2,1)S(1)}, bf16[1,1,32,3072]{3,2,1,0:T(8,128)(2,1)}, u32[]{:S(2)}) %copy-start) | copy-done | bytes 196632
  2.3 0.0 copy-start.1
  2.3 0.9 %copy-done.1 = bf16[1,1,32,3072]{3,2,1,0:T(8,128)(2,1)S(1)} copy-done((bf16[1,1,32,3072]{3,2,1,0:T(8,128)(2,1)S(1)}, bf16[1,1,32,3072]{3,2,1,0:T(8,128)(2,1)}, u32[]{:S(2)}) %copy-start.1) | copy-done | bytes 196632
  3.3 0.0 copy-start.2
  3.3 0.9 %copy-done.2 = bf16[1,1,32,3072]{3,2,1,0:T(8,128)(2,1)S(1)} copy-done((bf16[1,1,32,3072]{3,2,1,0:T(8,128)(2,1)S(1)}, bf16[1,1,32,3072]{3,2,1,0:T(8,128)(2,1)}, u32[]{:S(2)}) %copy-start.2) | copy-done | bytes 196632
  4.2 0.0 copy-start.3
  4.2 0.9 %copy-done.3 = bf16[1,1,32,3072]{3,2,1,0:T(8,128)(2,1)S(1)} copy-done((bf16[1,1,32,3072]{3,2,1,0:T(8,128)(2,1)S(1)}, bf16[1,1,32,3072]{3,2,1,0:T(8,128)(2,1)}, u32[]{:S(2)}) %copy-start.3) | copy-done | bytes 196632
  5.1 0.0 copy-start.4
  5.1 0.9 %copy-done.4 = bf16[1,1,32,3072]{3,2,1,0:T(8,128)(2,1)S(1)} copy-done((bf16[1,1,32,3072]{3,2,1,0:T(8,128)(2,1)S(1)}, bf16[1,1,32,3072]{3,2,1,0:T(8,128)(2,1)}, u32[]{:S(2)}) %copy-start.4) | copy-done | bytes 196632
  6.0 62.3 %shard_map.85 = bf16[3,32,3072]{2,1,0:T(8,128)(2,1)S(1)} custom-call(bf16[32,3072]{1,0:T(8,128)(2,1)S(1)} %bitcast.12, bf16[32,3072]{1,0:T(8,128)(2,1)S(1)} %bitcast.13, bf16[32,3072]{1,0:T(8,128)(2,1)S(1)} %bitcast.14, bf16[32,3072]{1,0:T(8,128)(2,1)S(1)} %bitcast.15, bf16[32,3072]{1,0:T(8,128)(2,1)S(1)} %bitcast.16, f32[32,24]{1,0:T(8,128)S(1)} %bitcast.17), custom_call_target="tpu_custom_call" | custom-call | tf_op jit(solution)/shard_map/pallas_call | solution.py:313
  68.4 0.8 %slice_bitcast_fusion = (bf16[1,1,32,3072]{3,2,1,0:T(8,128)(2,1)}, bf16[1,1,32,3072]{3,2,1,0:T(8,128)(2,1)}, bf16[1,1,32,3072]{3,2,1,0:T(8,128)(2,1)}) fusion(bf16[3,32,3072]{2,1,0:T(8,128)(2,1)S(1)} %shard_map.85), kind=kLoop, calls=%fused_computation | loop fusion | bytes 1179648 | tf_op jit(solution)/shard_map/reshape;squeeze | solution.py:350
Async XLA Ops:
  1.4 0.9 %copy-start = (bf16[1,1,32,3072]{3,2,1,0:T(8,128)(2,1)S(1)}, bf16[1,1,32,3072]{3,2,1,0:T(8,128)(2,1)}, u32[]{:S(2)}) copy-start(bf16[1,1,32,3072]{3,2,1,0:T(8,128)(2,1)} %param.6) | copy-start | bytes 589828
  2.3 0.9 %copy-start.1 = (bf16[1,1,32,3072]{3,2,1,0:T(8,128)(2,1)S(1)}, bf16[1,1,32,3072]{3,2,1,0:T(8,128)(2,1)}, u32[]{:S(2)}) copy-start(bf16[1,1,32,3072]{3,2,1,0:T(8,128)(2,1)} %param.7) | copy-start | bytes 589828
  3.3 0.9 %copy-start.2 = (bf16[1,1,32,3072]{3,2,1,0:T(8,128)(2,1)S(1)}, bf16[1,1,32,3072]{3,2,1,0:T(8,128)(2,1)}, u32[]{:S(2)}) copy-start(bf16[1,1,32,3072]{3,2,1,0:T(8,128)(2,1)} %param.8) | copy-start | bytes 589828
  4.2 0.9 %copy-start.3 = (bf16[1,1,32,3072]{3,2,1,0:T(8,128)(2,1)S(1)}, bf16[1,1,32,3072]{3,2,1,0:T(8,128)(2,1)}, u32[]{:S(2)}) copy-start(bf16[1,1,32,3072]{3,2,1,0:T(8,128)(2,1)} %param.9) | copy-start | bytes 589828
  5.1 0.9 %copy-start.4 = (bf16[1,1,32,3072]{3,2,1,0:T(8,128)(2,1)S(1)}, bf16[1,1,32,3072]{3,2,1,0:T(8,128)(2,1)}, u32[]{:S(2)}) copy-start(bf16[1,1,32,3072]{3,2,1,0:T(8,128)(2,1)} %param.10) | copy-start | bytes 589828

commit v2 on v1

--- a/solution.py
+++ b/solution.py
@@ -21,16 +21,19 @@
     nh, nw, nd, heads, tok,
     q_hbm, k_hbm, v_hbm, o_hbm, g_hbm, n_hbm,
     res,
-    xin, o_in, n_in, qd, kv, pad, st_out, st_in, st,
-    k_t, dq_acc, kv_acc, rq_send, rq_recv, rk_send, rk_recv, out_send,
+    xin, o_in, n_in, n_out, qd, kv, pad, st_out, st_in, st,
+    k_t, dq_acc, kv_acc, rq_send, rq_recv, rk_send, rk_recv, out_send, relay,
     sem_load, s_in, r_in, s_st, r_st, s_z, r_z, s_x, r_x, s_sz, r_sz,
-    s_rq, r_rq, s_rk, r_rk, s_out, r_out,
+    s_rq, r_rq, s_rk, r_rk, s_out, r_out, s_relay, r_relay,
 ):
     ih, iw, me = lax.axis_index("ha"), lax.axis_index("wa"), lax.axis_index("hd")
     tile = nd * tok
     scale = HD ** -0.5
     sides_h = (("ha", ih > 0, ih - 1, 0, 2), ("ha", ih < nh - 1, ih + 1, 2, 0))
     sides_w = (("wa", iw > 0, iw - 1, 0, 2), ("wa", iw < nw - 1, iw + 1, 2, 0))
+    mid = nw // 2
+    detours = ((mid - 1, 0, mid, 0), (mid, nw - 1, mid - 1, 2))
+    at_mid, at_end = (iw == mid - 1) | (iw == mid), (iw == 0) | (iw == nw - 1)
 
     barrier = pltpu.get_barrier_semaphore()
 
@@ -43,6 +46,11 @@
         @pl.when(exists)
         def _():
             pl.semaphore_signal(barrier, inc=1, device_id={axis: other}, device_id_type=MESH)
+    for there, others in ((at_mid, (0, nw - 1)), (at_end, (mid - 1, mid))):
+        @pl.when(there)
+        def _():
+            for other in others:
+                pl.semaphore_signal(barrier, inc=1, device_id={"wa": other}, device_id_type=MESH)
 
     loads = [
         pltpu.make_async_copy(src, dst, sem_load.at[n])
@@ -71,6 +79,7 @@
     count = jnp.int32(nd - 1)
     for _, exists, _, _, _ in sides_h + sides_w:
         count = count + exists.astype(jnp.int32)
+    count = count + 2 * (at_mid | at_end).astype(jnp.int32)
     pl.semaphore_wait(barrier, count)
 
     my_rows = pl.ds(pl.multiple_of(me * tok, tok), tok)
@@ -102,16 +111,16 @@
         load.wait()
     lane = lax.broadcasted_iota(jnp.int32, (tok, 128), 1)
     table = jnp.zeros((tok, 128), F32)
-    norms = n_in[...]
+    n_out[...] = jnp.zeros(n_out.shape, F32)
     for g in range(nd * heads):
         d, h = g // heads, g % heads
         cols = slice(g * HD, (g + 1) * HD)
         dots = jnp.sum(xin[1, :, cols].astype(F32) * o_in[:, cols].astype(F32), axis=1, keepdims=True)
-        table = jnp.where(lane == 8 * d + h, norms[:, g:g + 1], table)
+        n_out[8 * d + h:8 * d + h + 1, :tok] = n_in[g:g + 1, :]
         table = jnp.where(lane == 8 * d + heads + h, dots, table)
     pad[...] = jnp.zeros(pad.shape, F32)
     pad[pl.ds(pl.multiple_of(lax.rem(me, 4) * tok, tok), tok), :] = table
-    st_out[...] = pad[...].T
+    st_out[...] = pad[...].T[:64] + pltpu.roll(n_out[...], lax.rem(me, 4) * tok, 1)
 
     def spread_stats(t, c):
         d = lax.rem(me + 1 + t, nd)
@@ -134,6 +143,41 @@
             device_id={axis: other}, device_id_type=MESH,
         )
 
+    def seam(side):
+        return at_mid & (side[2] == (2 * mid - 1) - iw)
+
+    def leg(src, dst, send, recv, to):
+        return pltpu.make_async_remote_copy(
+            src_ref=src, dst_ref=dst, send_sem=send, recv_sem=recv,
+            device_id={"wa": to}, device_id_type=MESH,
+        )
+
+    def send_kv(h, side, src, dst, send, recv, trip):
+        @pl.when(side[1] & jnp.logical_not(seam(side)))
+        def _():
+            leg(src, dst, send, recv, side[2]).start()
+
+        @pl.when(side[1] & seam(side))
+        def _():
+            leg(src.at[0], dst.at[0], send, recv, side[2]).start()
+            leg(src.at[1], relay.at[trip, h], send, r_relay.at[trip, h], detour_of(side)).start()
+
+    def detour_of(side):
+        return jnp.where(iw == mid - 1, detours[0][1], detours[1][1])
+
+    def pass_on(h, buf_of, sem_of, trip):
+        for _, via, target, there in detours:
+            @pl.when(iw == via)
+            def _():
+                pltpu.make_async_copy(relay.at[trip, h], relay.at[trip, h], r_relay.at[trip, h]).wait()
+                leg(relay.at[trip, h], buf_of(there).at[1], s_relay.at[trip, h], sem_of(there), target).start()
+
+    def pass_kv(h):
+        pass_on(h, lambda there: kv.at[there, h], lambda there: r_x.at[h, there // 2], 0)
+
+    def pass_back(h):
+        pass_on(h, lambda there: rk_recv.at[there // 2, h], lambda there: r_rk.at[there // 2, h], 1)
+
     def halo_stats(side):
         axis, _, other, slot, there = side
         return pltpu.make_async_remote_copy(
@@ -153,7 +197,9 @@
             when(side, lambda: halo(qd, h, side, s_z, r_z).start())
         pltpu.make_async_copy(kv.at[1, h], kv.at[1, h], r_in.at[h, 1]).wait()
         for side in sides_w:
-            when(side, lambda: halo(kv, h, side, s_x, r_x).start())
+            send_kv(h, side, kv.at[1, h], kv.at[side[4], h], s_x.at[h, side[3] // 2], r_x.at[h, side[4] // 2], 0)
+        if h > 0:
+            pass_kv(h - 1)
         if h == 0:
             pltpu.make_async_copy(st_in, st_in, r_st.at[0]).wait()
             got = st_in[...]
@@ -162,6 +208,8 @@
             )
             for side in sides_h:
                 when(side, lambda: halo_stats(side).start())
+
+    pass_kv(heads - 1)
 
     def arrived(buf, slot, h, sem):
         pltpu.make_async_copy(buf.at[slot, h], buf.at[slot, h], sem.at[h, slot // 2]).wait()
@@ -231,7 +279,10 @@
         for side in sides_w:
             slot = side[3]
             rk_send[slot // 2, h] = kv_acc[h, slot].astype(BF16)
-            when(side, lambda: back_kv(h, side).start())
+            send_kv(
+                h, side, rk_send.at[slot // 2, h], rk_recv.at[side[4] // 2, h],
+                s_rk.at[slot // 2, h], r_rk.at[side[4] // 2, h], 1,
+            )
 
     def finish(h):
         for n, side in enumerate(sides_h):
@@ -263,11 +314,17 @@
 
         @pl.when(h > 0)
         def _():
-            finish(h - 1)
+            pass_back(h - 1)
         return c
 
     lax.fori_loop(0, heads, step, 0)
-    finish(heads - 1)
+    pass_back(heads - 1)
+
+    def close(h, c):
+        finish(h)
+        return c
+
+    lax.fori_loop(0, heads, close, 0)
 
     def drain(t, c):
         d = lax.rem(me + 1 + t, nd)
@@ -291,6 +348,11 @@
         for side in sides_w:
             when(side, lambda: halo(kv, h, side, s_x, r_x).wait_send())
             when(side, lambda: back_kv(h, side).wait_send())
+
+        @pl.when(at_end)
+        def _():
+            for trip in range(2):
+                pltpu.make_async_copy(relay.at[trip, h], relay.at[trip, h], s_relay.at[trip, h]).wait()
     for h in range(heads):
         part = res.at[:, :, pl.ds(0, nd * HD)]
         pltpu.make_async_copy(part, part, r_out.at[h]).wait()
@@ -313,16 +375,17 @@
         res = pl.pallas_call(
             kernel,
             out_shape=jax.ShapeDtypeStruct((3, tok, chan), BF16),
-            in_specs=[pl.BlockSpec(memory_space=pl.ANY)] * 6,
-            out_specs=pl.BlockSpec(memory_space=pltpu.VMEM),
+            in_specs=[pl.BlockSpec(memory_space=pltpu.HBM)] * 6,
+            out_specs=pl.BlockSpec(memory_space=pltpu.HBM),
             scratch_shapes=[
                 pltpu.VMEM((4, tok, chan), BF16),
                 pltpu.VMEM((tok, chan), BF16),
-                pltpu.VMEM((tok, n.shape[3]), F32),
+                pltpu.VMEM((n.shape[3], tok), F32),
+                pltpu.VMEM((64, 128), F32),
                 pltpu.VMEM((3, heads, 2, tile, HD), BF16),
                 pltpu.VMEM((3, heads, 2, tile, HD), BF16),
                 pltpu.VMEM((128, 128), F32),
-                pltpu.VMEM((128, 128), F32),
+                pltpu.VMEM((64, 128), F32),
                 pltpu.VMEM((nd, 8, 128), F32),
                 pltpu.VMEM((3, 8, tile), F32),
                 pltpu.VMEM((3, HD, tile), BF16),
@@ -333,6 +396,7 @@
                 pltpu.VMEM((2, heads, 2, tile, HD), BF16),
                 pltpu.VMEM((2, heads, 2, tile, HD), BF16),
                 pltpu.VMEM((heads, 3, tile, HD), BF16),
+                pltpu.VMEM((2, heads, tile, HD), BF16),
                 dma((6,)),
                 dma((heads, 2, nd - 1)), dma((heads, 2)),
                 dma((nd - 1,)), dma((1,)),
@@ -342,11 +406,12 @@
                 dma((2, heads)), dma((2, heads)),
                 dma((2, heads)), dma((2, heads)),
                 dma((heads, nd - 1)), dma((heads,)),
+                dma((2, heads)), dma((2, heads)),
             ],
             compiler_params=pltpu.CompilerParams(
-                collective_id=0, has_side_effects=True, vmem_limit_bytes=48 * 1024 * 1024
+                collective_id=0, has_side_effects=True, vmem_limit_bytes=60 * 1024 * 1024
             ),
-        )(*(x.reshape(x.shape[2:]) for x in (q, k, v, o, g, n)))
+        )(*(x.reshape(x.shape[2:]) for x in (q, k, v, o, g)), n.reshape(n.shape[2:]).T)
         return tuple(res[i].reshape(lead) for i in range(3))
 
     return jax.shard_map(

time: 69.5 us -> 58.2 us (0.84); the launches traced: 69.2 us -> 57.2 us
  Pallas kernels: 62.3 us -> 54.6 us
  local copies, waits for them, and re-layouts: 6.23 us -> 1.94 us
    pallas_call x1, Pallas kernels: 62.3 us -> 54.6 us  [per_device(): pl.pallas_call(kernel, out_shape=jax.ShapeDtypeStruct((3, tok, chan), BF1...]
    unnamed x11 -> x0, local copies, waits for them, and re-layouts: 5.41 us -> none
    another operation x1, local copies, waits for them, and re-layouts: 0.82 us -> 1.94 us  [per_device(): return tuple((res[i].reshape(lead) for i in range(3)))]
where the time goes in v2:
time: 58.2 us; the launch traced here: 57.2 us
  Pallas kernels  54.6 us (94%)
  local copies, waits for them, and re-layouts  1.94 us (3%)
  between operations  0.64 us (1%)
    pallas_call x1, Pallas kernels, per_device(): pl.pallas_call(kernel, out_shape=jax.ShapeDtypeStruct((3, tok, chan), BF1...  54.6 us
    another operation x1, local copies, waits for them, and re-layouts, per_device(): return tuple((res[i].reshape(lead) for i in range(3)))  1.94 us

profile of v2, /device:TPU:71, one launch (start us, length us, event | category | flops | bytes accessed | tf_op | source)
XLA Modules:
  0.0 57.2 jit_solution(15817056006503946606)
XLA Ops:
  0.6 54.6 %shard_map.85 = bf16[3,32,3072]{2,1,0:T(8,128)(2,1)} custom-call(bf16[32,3072]{1,0:T(8,128)(2,1)} %bitcast.14, bf16[32,3072]{1,0:T(8,128)(2,1)} %bitcast.15, bf16[32,3072]{1,0:T(8,128)(2,1)} %bitcast.16, bf16[32,3072]{1,0:T(8,128)(2,1)} %bitcast.17, bf16[32,3072]{1,0:T(8,128)(2,1)} %bitcast.18, f32[24,32]{1,0:T(8,128)} %bitcast.19), custom_call_target="tpu_custom_call" | custom-call | tf_op jit(solution)/shard_map/pallas_call | solution.py:375
  55.2 1.9 %slice_bitcast_fusion = (bf16[1,1,32,3072]{3,2,1,0:T(8,128)(2,1)}, bf16[1,1,32,3072]{3,2,1,0:T(8,128)(2,1)}, bf16[1,1,32,3072]{3,2,1,0:T(8,128)(2,1)}) fusion(bf16[3,32,3072]{2,1,0:T(8,128)(2,1)} %shard_map.85), kind=kLoop, calls=%fused_computation | loop fusion | bytes 1179648 | tf_op jit(solution)/shard_map/reshape;squeeze | solution.py:415

commit v3 on v2

--- a/solution.py
+++ b/solution.py
@@ -6,6 +6,7 @@
 from jax.sharding import PartitionSpec as P
 
 HD = 128
+FAR = ((1, 1, 1), (1, 1, 1))
 MESH = pl.DeviceIdType.MESH
 F32 = jnp.float32
 BF16 = jnp.bfloat16
@@ -22,9 +23,9 @@
     q_hbm, k_hbm, v_hbm, o_hbm, g_hbm, n_hbm,
     res,
     xin, o_in, n_in, n_out, qd, kv, pad, st_out, st_in, st,
-    k_t, dq_acc, kv_acc, rq_send, rq_recv, rk_send, rk_recv, out_send, relay,
+    k_t, dq_acc, kv_acc, rq_send, rq_recv, rk_send, rk_recv, out_send, relay, raw,
     sem_load, s_in, r_in, s_st, r_st, s_z, r_z, s_x, r_x, s_sz, r_sz,
-    s_rq, r_rq, s_rk, r_rk, s_out, r_out, s_relay, r_relay,
+    s_rq, r_rq, s_rk, r_rk, s_out, r_out, s_relay, r_relay, s_raw, r_raw, s_spread,
 ):
     ih, iw, me = lax.axis_index("ha"), lax.axis_index("wa"), lax.axis_index("hd")
     tile = nd * tok
@@ -82,11 +83,16 @@
     count = count + 2 * (at_mid | at_end).astype(jnp.int32)
     pl.semaphore_wait(barrier, count)
 
+    def when(side, fn):
+        @pl.when(side[1])
+        def _():
+            fn()
+
     my_rows = pl.ds(pl.multiple_of(me * tok, tok), tok)
 
     def spread(h, part, dst):
         def lanes(d):
-            return pl.ds(pl.multiple_of(d * (heads * HD) + h * HD, HD), HD)
+            return pl.ds(pl.multiple_of((h * nd + d) * HD, HD), HD)
 
         def one(t, c):
             d = lax.rem(me + 1 + t, nd)
@@ -103,9 +109,19 @@
             xin.at[pl.ds(2 * part, 2), :, lanes(me)], dst.at[1, h, :, my_rows, :], r_in.at[h, part]
         ).start()
 
-    for h in range(heads):
-        spread(h, 0, qd)
-        spread(h, 1, kv)
+    def raw_halo(side):
+        axis, _, other, slot, there = side
+        return pltpu.make_async_remote_copy(
+            src_ref=xin.at[pl.ds(0, 2), :, pl.ds(0, nd * HD)], dst_ref=raw.at[there // 2],
+            send_sem=s_raw.at[slot // 2], recv_sem=r_raw.at[there // 2],
+            device_id={axis: other}, device_id_type=MESH,
+        )
+
+    for side in sides_h:
+        when(side, lambda: raw_halo(side).start())
+    spread(1, 0, qd)
+    spread(0, 1, kv)
+    spread(0, 0, qd)
 
     for load in loads[4:]:
         load.wait()
@@ -113,7 +129,7 @@
     table = jnp.zeros((tok, 128), F32)
     n_out[...] = jnp.zeros(n_out.shape, F32)
     for g in range(nd * heads):
-        d, h = g // heads, g % heads
+        h, d = g // nd, g % nd
         cols = slice(g * HD, (g + 1) * HD)
         dots = jnp.sum(xin[1, :, cols].astype(F32) * o_in[:, cols].astype(F32), axis=1, keepdims=True)
         n_out[8 * d + h:8 * d + h + 1, :tok] = n_in[g:g + 1, :]
@@ -159,18 +175,34 @@
 
         @pl.when(side[1] & seam(side))
         def _():
-            leg(src.at[0], dst.at[0], send, recv, side[2]).start()
-            leg(src.at[1], relay.at[trip, h], send, r_relay.at[trip, h], detour_of(side)).start()
+            for n in range(heads):
+                @pl.when(h == n)
+                def _():
+                    near, far = shares(n, trip)
+                    if near is not None:
+                        leg(src.at[near], dst.at[near], send, recv, side[2]).start()
+                    if far is not None:
+                        leg(
+                            src.at[far], relay.at[trip, n].at[far], send, r_relay.at[trip, n], detour_of(side)
+                        ).start()
+
+    def shares(h, trip):
+        far = FAR[trip][h]
+        return (pl.ds(0, 2 - far) if far < 2 else None), (pl.ds(2 - far, far) if far else None)
 
     def detour_of(side):
         return jnp.where(iw == mid - 1, detours[0][1], detours[1][1])
 
     def pass_on(h, buf_of, sem_of, trip):
+        far = shares(h, trip)[1]
+        if far is None:
+            return
+        held = relay.at[trip, h].at[far]
         for _, via, target, there in detours:
             @pl.when(iw == via)
             def _():
-                pltpu.make_async_copy(relay.at[trip, h], relay.at[trip, h], r_relay.at[trip, h]).wait()
-                leg(relay.at[trip, h], buf_of(there).at[1], s_relay.at[trip, h], sem_of(there), target).start()
+                pltpu.make_async_copy(held, held, r_relay.at[trip, h]).wait()
+                leg(held, buf_of(there).at[far], s_relay.at[trip, h], sem_of(there), target).start()
 
     def pass_kv(h):
         pass_on(h, lambda there: kv.at[there, h], lambda there: r_x.at[h, there // 2], 0)
@@ -186,29 +218,61 @@
             device_id={axis: other}, device_id_type=MESH,
         )
 
-    def when(side, fn):
-        @pl.when(side[1])
-        def _():
-            fn()
-
-    for h in range(heads):
-        pltpu.make_async_copy(qd.at[1, h], qd.at[1, h], r_in.at[h, 0]).wait()
+    def spread_raw(side):
+        n = side[3] // 2
+        pltpu.make_async_copy(raw.at[n], raw.at[n], r_raw.at[n]).wait()
+
+        def one(t, c):
+            d = lax.rem(me + 1 + t, nd)
+            pltpu.make_async_remote_copy(
+                src_ref=raw.at[n, :, :, pl.ds(pl.multiple_of(d * HD, HD), HD)],
+                dst_ref=qd.at[side[3], 0, :, my_rows, :],
+                send_sem=s_spread.at[n, t], recv_sem=r_z.at[0, n],
+                device_id={"hd": d}, device_id_type=MESH,
+            ).start()
+            return c
+
+        lax.fori_loop(0, nd - 1, one, 0)
+        pltpu.make_async_copy(
+            raw.at[n, :, :, pl.ds(pl.multiple_of(me * HD, HD), HD)],
+            qd.at[side[3], 0, :, my_rows, :], r_z.at[0, n],
+        ).start()
+
+    def own(buf, h, part):
+        pltpu.make_async_copy(buf.at[1, h], buf.at[1, h], r_in.at[h, part]).wait()
+
+    def send_rows(h):
+        own(qd, h, 0)
         for side in sides_h:
             when(side, lambda: halo(qd, h, side, s_z, r_z).start())
-        pltpu.make_async_copy(kv.at[1, h], kv.at[1, h], r_in.at[h, 1]).wait()
+
+    def send_columns(h):
+        own(kv, h, 1)
         for side in sides_w:
             send_kv(h, side, kv.at[1, h], kv.at[side[4], h], s_x.at[h, side[3] // 2], r_x.at[h, side[4] // 2], 0)
-        if h > 0:
-            pass_kv(h - 1)
-        if h == 0:
-            pltpu.make_async_copy(st_in, st_in, r_st.at[0]).wait()
-            got = st_in[...]
-            st[1] = jnp.concatenate(
-                [got[0] + got[1] + got[2] + got[3], got[4] + got[5] + got[6] + got[7]], axis=1
-            )
+
+    send_rows(1)
+    for h in range(2, heads):
+        spread(h, 0, qd)
+    for h in range(1, heads):
+        spread(h, 1, kv)
+    send_columns(0)
+    pltpu.make_async_copy(st_in, st_in, r_st.at[0]).wait()
+    got = st_in[...]
+    st[1] = jnp.concatenate(
+        [got[0] + got[1] + got[2] + got[3], got[4] + got[5] + got[6] + got[7]], axis=1
+    )
+    for side in sides_h:
+        when(side, lambda: halo_stats(side).start())
+    for h in range(2, heads):
+        send_rows(h)
+    for h in range(1, heads):
+        send_columns(h)
+        if h == 1:
             for side in sides_h:
-                when(side, lambda: halo_stats(side).start())
-
+                when(side, lambda: spread_raw(side))
+            own(qd, 0, 0)
+        pass_kv(h - 1)
     pass_kv(heads - 1)
 
     def arrived(buf, slot, h, sem):
@@ -234,7 +298,7 @@
         d = lax.rem(me + 1 + t, nd)
         return pltpu.make_async_remote_copy(
             src_ref=out_send.at[h, :, pl.ds(pl.multiple_of(d * tok, tok), tok), :],
-            dst_ref=res.at[:, :, pl.ds(pl.multiple_of(me * (heads * HD) + h * HD, HD), HD)],
+            dst_ref=res.at[:, :, pl.ds(pl.multiple_of((h * nd + me) * HD, HD), HD)],
             send_sem=s_out.at[h, t], recv_sem=r_out.at[h],
             device_id={"hd": d}, device_id_type=MESH,
         )
@@ -305,16 +369,17 @@
         lax.fori_loop(0, nd - 1, one, 0)
         pltpu.make_async_copy(
             out_send.at[h, :, my_rows, :],
-            res.at[:, :, pl.ds(pl.multiple_of(me * (heads * HD) + h * HD, HD), HD)],
+            res.at[:, :, pl.ds(pl.multiple_of((h * nd + me) * HD, HD), HD)],
             r_out.at[h],
         ).start()
 
     def step(h, c):
         compute(h)
 
-        @pl.when(h > 0)
-        def _():
-            pass_back(h - 1)
+        for n in range(1, heads):
+            @pl.when(h == n)
+            def _():
+                pass_back(n - 1)
         return c
 
     lax.fori_loop(0, heads, step, 0)
@@ -339,11 +404,22 @@
         return c
 
     lax.fori_loop(0, nd - 1, drain, 0)
+    def drain_raw(side):
+        def one(t, c):
+            src = raw.at[side[3] // 2, :, :, pl.ds(0, HD)]
+            pltpu.make_async_copy(src, src, s_spread.at[side[3] // 2, t]).wait()
+            return c
+
+        raw_halo(side).wait_send()
+        lax.fori_loop(0, nd - 1, one, 0)
+
     for side in sides_h:
         when(side, lambda: halo_stats(side).wait_send())
+        when(side, lambda: drain_raw(side))
     for h in range(heads):
         for side in sides_h:
-            when(side, lambda: halo(qd, h, side, s_z, r_z).wait_send())
+            if h > 0:
+                when(side, lambda: halo(qd, h, side, s_z, r_z).wait_send())
             when(side, lambda: back_q(h, side).wait_send())
         for side in sides_w:
             when(side, lambda: halo(kv, h, side, s_x, r_x).wait_send())
@@ -352,7 +428,10 @@
         @pl.when(at_end)
         def _():
             for trip in range(2):
-                pltpu.make_async_copy(relay.at[trip, h], relay.at[trip, h], s_relay.at[trip, h]).wait()
+                far = shares(h, trip)[1]
+                if far is not None:
+                    held = relay.at[trip, h].at[far]
+                    pltpu.make_async_copy(held, held, s_relay.at[trip, h]).wait()
     for h in range(heads):
         part = res.at[:, :, pl.ds(0, nd * HD)]
         pltpu.make_async_copy(part, part, r_out.at[h]).wait()
@@ -396,7 +475,8 @@
                 pltpu.VMEM((2, heads, 2, tile, HD), BF16),
                 pltpu.VMEM((2, heads, 2, tile, HD), BF16),
                 pltpu.VMEM((heads, 3, tile, HD), BF16),
-                pltpu.VMEM((2, heads, tile, HD), BF16),
+                pltpu.VMEM((2, heads, 2, tile, HD), BF16),
+                pltpu.VMEM((2, 2, tok, nd * HD), BF16),
                 dma((6,)),
                 dma((heads, 2, nd - 1)), dma((heads, 2)),
                 dma((nd - 1,)), dma((1,)),
@@ -407,6 +487,7 @@
                 dma((2, heads)), dma((2, heads)),
                 dma((heads, nd - 1)), dma((heads,)),
                 dma((2, heads)), dma((2, heads)),
+                dma((2,)), dma((2,)), dma((2, nd - 1)),
             ],
             compiler_params=pltpu.CompilerParams(
                 collective_id=0, has_side_effects=True, vmem_limit_bytes=60 * 1024 * 1024

time: 58.2 us -> 54 us (0.928); the launches traced: 57.2 us -> 53.9 us
  Pallas kernels: 54.6 us -> 51.3 us
    pallas_call x1, Pallas kernels: 54.6 us -> 51.3 us  [per_device(): pl.pallas_call(kernel, out_shape=jax.ShapeDtypeStruct((3, tok, chan), BF1...]
where the time goes in v3:
time: 54 us; the launch traced here: 53.9 us
  Pallas kernels  51.3 us (95%)
  local copies, waits for them, and re-layouts  1.94 us (4%)
  between operations  0.64 us (1%)
    pallas_call x1, Pallas kernels, per_device(): pl.pallas_call(kernel, out_shape=jax.ShapeDtypeStruct((3, tok, chan), BF1...  51.3 us
    another operation x1, local copies, waits for them, and re-layouts, per_device(): return tuple((res[i].reshape(lead) for i in range(3)))  1.94 us

profile of v3, /device:TPU:71, one launch (start us, length us, event | category | flops | bytes accessed | tf_op | source)
XLA Modules:
  0.0 53.9 jit_solution(13541597199850254289)
XLA Ops:
  0.6 51.3 %shard_map.85 = bf16[3,32,3072]{2,1,0:T(8,128)(2,1)} custom-call(bf16[32,3072]{1,0:T(8,128)(2,1)} %bitcast.14, bf16[32,3072]{1,0:T(8,128)(2,1)} %bitcast.15, bf16[32,3072]{1,0:T(8,128)(2,1)} %bitcast.16, bf16[32,3072]{1,0:T(8,128)(2,1)} %bitcast.17, bf16[32,3072]{1,0:T(8,128)(2,1)} %bitcast.18, f32[24,32]{1,0:T(8,128)} %bitcast.19), custom_call_target="tpu_custom_call" | custom-call | tf_op jit(solution)/shard_map/pallas_call | solution.py:454
  51.9 1.9 %slice_bitcast_fusion = (bf16[1,1,32,3072]{3,2,1,0:T(8,128)(2,1)}, bf16[1,1,32,3072]{3,2,1,0:T(8,128)(2,1)}, bf16[1,1,32,3072]{3,2,1,0:T(8,128)(2,1)}) fusion(bf16[3,32,3072]{2,1,0:T(8,128)(2,1)} %shard_map.85), kind=kLoop, calls=%fused_computation | loop fusion | bytes 1179648 | tf_op jit(solution)/shard_map/reshape;squeeze | solution.py:496

commit v4 on v3

--- a/solution.py
+++ b/solution.py
@@ -6,7 +6,7 @@
 from jax.sharding import PartitionSpec as P
 
 HD = 128
-FAR = ((1, 1, 1), (1, 1, 1))
+ROUTES = (((0, 1), (0, 1), (0, 1)), ((0, 1), (0, 1), (0, 1)))
 MESH = pl.DeviceIdType.MESH
 F32 = jnp.float32
 BF16 = jnp.bfloat16
@@ -33,8 +33,10 @@
     sides_h = (("ha", ih > 0, ih - 1, 0, 2), ("ha", ih < nh - 1, ih + 1, 2, 0))
     sides_w = (("wa", iw > 0, iw - 1, 0, 2), ("wa", iw < nw - 1, iw + 1, 2, 0))
     mid = nw // 2
-    detours = ((mid - 1, 0, mid, 0), (mid, nw - 1, mid - 1, 2))
-    at_mid, at_end = (iw == mid - 1) | (iw == mid), (iw == 0) | (iw == nw - 1)
+    vias = (0, 1, 2)
+    at_mid = (iw == mid - 1) | (iw == mid)
+    detours = lambda r: ((mid - 1, vias[r - 1], mid, 0), (mid, nw - 1 - vias[r - 1], mid - 1, 2))
+    met = [(m, v) for m in (mid - 1, mid) for w in vias for v in (w, nw - 1 - w) if abs(m - v) > 1]
 
     barrier = pltpu.get_barrier_semaphore()
 
@@ -47,10 +49,10 @@
         @pl.when(exists)
         def _():
             pl.semaphore_signal(barrier, inc=1, device_id={axis: other}, device_id_type=MESH)
-    for there, others in ((at_mid, (0, nw - 1)), (at_end, (mid - 1, mid))):
-        @pl.when(there)
-        def _():
-            for other in others:
+    for m, v in met:
+        for here, other in ((m, v), (v, m)):
+            @pl.when(iw == here)
+            def _():
                 pl.semaphore_signal(barrier, inc=1, device_id={"wa": other}, device_id_type=MESH)
 
     loads = [
@@ -80,7 +82,8 @@
     count = jnp.int32(nd - 1)
     for _, exists, _, _, _ in sides_h + sides_w:
         count = count + exists.astype(jnp.int32)
-    count = count + 2 * (at_mid | at_end).astype(jnp.int32)
+    for m, v in met:
+        count = count + ((iw == m) | (iw == v)).astype(jnp.int32)
     pl.semaphore_wait(barrier, count)
 
     def when(side, fn):
@@ -119,8 +122,8 @@
 
     for side in sides_h:
         when(side, lambda: raw_halo(side).start())
+    spread(0, 1, kv)
     spread(1, 0, qd)
-    spread(0, 1, kv)
     spread(0, 0, qd)
 
     for load in loads[4:]:
@@ -178,31 +181,26 @@
             for n in range(heads):
                 @pl.when(h == n)
                 def _():
-                    near, far = shares(n, trip)
-                    if near is not None:
-                        leg(src.at[near], dst.at[near], send, recv, side[2]).start()
-                    if far is not None:
-                        leg(
-                            src.at[far], relay.at[trip, n].at[far], send, r_relay.at[trip, n], detour_of(side)
-                        ).start()
-
-    def shares(h, trip):
-        far = FAR[trip][h]
-        return (pl.ds(0, 2 - far) if far < 2 else None), (pl.ds(2 - far, far) if far else None)
-
-    def detour_of(side):
-        return jnp.where(iw == mid - 1, detours[0][1], detours[1][1])
+                    for part, r in enumerate(ROUTES[trip][n]):
+                        if r == 0:
+                            leg(src.at[part], dst.at[part], send, recv, side[2]).start()
+                        else:
+                            up, down = detours(r)
+                            leg(
+                                src.at[part], relay.at[trip, n, part], send, r_relay.at[trip, n, part],
+                                jnp.where(iw == mid - 1, up[1], down[1]),
+                            ).start()
 
     def pass_on(h, buf_of, sem_of, trip):
-        far = shares(h, trip)[1]
-        if far is None:
-            return
-        held = relay.at[trip, h].at[far]
-        for _, via, target, there in detours:
-            @pl.when(iw == via)
-            def _():
-                pltpu.make_async_copy(held, held, r_relay.at[trip, h]).wait()
-                leg(held, buf_of(there).at[far], s_relay.at[trip, h], sem_of(there), target).start()
+        for part, r in enumerate(ROUTES[trip][h]):
+            if r == 0:
+                continue
+            held = relay.at[trip, h, part]
+            for _, via, target, there in detours(r):
+                @pl.when(iw == via)
+                def _():
+                    pltpu.make_async_copy(held, held, r_relay.at[trip, h, part]).wait()
+                    leg(held, buf_of(there).at[part], s_relay.at[trip, h, part], sem_of(there), target).start()
 
     def pass_kv(h):
         pass_on(h, lambda there: kv.at[there, h], lambda there: r_x.at[h, there // 2], 0)
@@ -251,12 +249,10 @@
         for side in sides_w:
             send_kv(h, side, kv.at[1, h], kv.at[side[4], h], s_x.at[h, side[3] // 2], r_x.at[h, side[4] // 2], 0)
 
+    send_columns(0)
     send_rows(1)
-    for h in range(2, heads):
-        spread(h, 0, qd)
-    for h in range(1, heads):
-        spread(h, 1, kv)
-    send_columns(0)
+    spread(1, 1, kv)
+    spread(2, 0, qd)
     pltpu.make_async_copy(st_in, st_in, r_st.at[0]).wait()
     got = st_in[...]
     st[1] = jnp.concatenate(
@@ -264,16 +260,16 @@
     )
     for side in sides_h:
         when(side, lambda: halo_stats(side).start())
-    for h in range(2, heads):
-        send_rows(h)
-    for h in range(1, heads):
-        send_columns(h)
-        if h == 1:
-            for side in sides_h:
-                when(side, lambda: spread_raw(side))
-            own(qd, 0, 0)
-        pass_kv(h - 1)
-    pass_kv(heads - 1)
+    own(qd, 0, 0)
+    for side in sides_h:
+        when(side, lambda: spread_raw(side))
+    spread(2, 1, kv)
+    pass_kv(0)
+    send_columns(1)
+    send_rows(2)
+    pass_kv(1)
+    send_columns(2)
+    pass_kv(2)
 
     def arrived(buf, slot, h, sem):
         pltpu.make_async_copy(buf.at[slot, h], buf.at[slot, h], sem.at[h, slot // 2]).wait()
@@ -375,18 +371,18 @@
 
     def step(h, c):
         compute(h)
-
-        for n in range(1, heads):
-            @pl.when(h == n)
-            def _():
-                pass_back(n - 1)
         return c
 
     lax.fori_loop(0, heads, step, 0)
-    pass_back(heads - 1)
+    for h in range(heads - 1):
+        pass_back(h)
 
     def close(h, c):
         finish(h)
+
+        @pl.when(h == 0)
+        def _():
+            pass_back(heads - 1)
         return c
 
     lax.fori_loop(0, heads, close, 0)
@@ -425,13 +421,15 @@
             when(side, lambda: halo(kv, h, side, s_x, r_x).wait_send())
             when(side, lambda: back_kv(h, side).wait_send())
 
-        @pl.when(at_end)
-        def _():
-            for trip in range(2):
-                far = shares(h, trip)[1]
-                if far is not None:
-                    held = relay.at[trip, h].at[far]
-                    pltpu.make_async_copy(held, held, s_relay.at[trip, h]).wait()
+        for trip in range(2):
+            for part, r in enumerate(ROUTES[trip][h]):
+                if r == 0:
+                    continue
+                held = relay.at[trip, h, part]
+                for _, via, _, _ in detours(r):
+                    @pl.when(iw == via)
+                    def _():
+                        pltpu.make_async_copy(held, held, s_relay.at[trip, h, part]).wait()
     for h in range(heads):
         part = res.at[:, :, pl.ds(0, nd * HD)]
         pltpu.make_async_copy(part, part, r_out.at[h]).wait()
@@ -486,7 +484,7 @@
                 dma((2, heads)), dma((2, heads)),
                 dma((2, heads)), dma((2, heads)),
                 dma((heads, nd - 1)), dma((heads,)),
-                dma((2, heads)), dma((2, heads)),
+                dma((2, heads, 2)), dma((2, heads, 2)),
                 dma((2,)), dma((2,)), dma((2, nd - 1)),
             ],
             compiler_params=pltpu.CompilerParams(

time: 54 us -> 53.3 us (0.987)
  Pallas kernels: 51.3 us -> 50.6 us
    pallas_call x1, Pallas kernels: 51.3 us -> 50.6 us  [per_device(): pl.pallas_call(kernel, out_shape=jax.ShapeDtypeStruct((3, tok, chan), BF1...]
where the time goes in v4:
time: 53.3 us; the launch traced here: 53.2 us
  Pallas kernels  50.6 us (95%)
  local copies, waits for them, and re-layouts  1.94 us (4%)
  between operations  0.64 us (1%)
    pallas_call x1, Pallas kernels, per_device(): pl.pallas_call(kernel, out_shape=jax.ShapeDtypeStruct((3, tok, chan), BF1...  50.6 us
    another operation x1, local copies, waits for them, and re-layouts, per_device(): return tuple((res[i].reshape(lead) for i in range(3)))  1.94 us

profile of v4, /device:TPU:71, one launch (start us, length us, event | category | flops | bytes accessed | tf_op | source)
XLA Modules:
  0.0 53.2 jit_solution(3785513924245663104)
XLA Ops:
  0.6 50.6 %shard_map.85 = bf16[3,32,3072]{2,1,0:T(8,128)(2,1)} custom-call(bf16[32,3072]{1,0:T(8,128)(2,1)} %bitcast.14, bf16[32,3072]{1,0:T(8,128)(2,1)} %bitcast.15, bf16[32,3072]{1,0:T(8,128)(2,1)} %bitcast.16, bf16[32,3072]{1,0:T(8,128)(2,1)} %bitcast.17, bf16[32,3072]{1,0:T(8,128)(2,1)} %bitcast.18, f32[24,32]{1,0:T(8,128)} %bitcast.19), custom_call_target="tpu_custom_call" | custom-call | tf_op jit(solution)/shard_map/pallas_call | solution.py:452
  51.2 1.9 %slice_bitcast_fusion = (bf16[1,1,32,3072]{3,2,1,0:T(8,128)(2,1)}, bf16[1,1,32,3072]{3,2,1,0:T(8,128)(2,1)}, bf16[1,1,32,3072]{3,2,1,0:T(8,128)(2,1)}) fusion(bf16[3,32,3072]{2,1,0:T(8,128)(2,1)} %shard_map.85), kind=kLoop, calls=%fused_computation | loop fusion | bytes 1179648 | tf_op jit(solution)/shard_map/reshape;squeeze | solution.py:494

commit v5 on v4

--- a/solution.py
+++ b/solution.py
@@ -451,9 +451,9 @@
         dma = pltpu.SemaphoreType.DMA
         res = pl.pallas_call(
             kernel,
-            out_shape=jax.ShapeDtypeStruct((3, tok, chan), BF16),
+            out_shape=pltpu.VMEM((3, tok, chan), BF16),
             in_specs=[pl.BlockSpec(memory_space=pltpu.HBM)] * 6,
-            out_specs=pl.BlockSpec(memory_space=pltpu.HBM),
+            out_specs=pl.BlockSpec(memory_space=pltpu.VMEM),
             scratch_shapes=[
                 pltpu.VMEM((4, tok, chan), BF16),
                 pltpu.VMEM((tok, chan), BF16),

time: 53.3 us -> 52.1 us (0.977)
  local copies, waits for them, and re-layouts: 1.94 us -> 0.82 us
    another operation x1, local copies, waits for them, and re-layouts: 1.94 us -> 0.82 us  [per_device(): return tuple((res[i].reshape(lead) for i in range(3)))]
where the time goes in v5:
time: 52.1 us; the launch traced here: 52 us
  Pallas kernels  50.5 us (97%)
  local copies, waits for them, and re-layouts  0.82 us (2%)
  between operations  0.64 us (1%)
    pallas_call x1, Pallas kernels, per_device(): pl.pallas_call(kernel, out_shape=pltpu.VMEM((3, tok, chan), BF16), in_spe...  50.5 us

profile of v5, /device:TPU:71, one launch (start us, length us, event | category | flops | bytes accessed | tf_op | source)
XLA Modules:
  0.0 52.0 jit_solution(12817238420275858886)
XLA Ops:
  0.6 50.5 %shard_map.85 = bf16[3,32,3072]{2,1,0:T(8,128)(2,1)S(1)} custom-call(bf16[32,3072]{1,0:T(8,128)(2,1)} %bitcast.14, bf16[32,3072]{1,0:T(8,128)(2,1)} %bitcast.15, bf16[32,3072]{1,0:T(8,128)(2,1)} %bitcast.16, bf16[32,3072]{1,0:T(8,128)(2,1)} %bitcast.17, bf16[32,3072]{1,0:T(8,128)(2,1)} %bitcast.18, f32[24,32]{1,0:T(8,128)} %bitcast.19), custom_call_target="tpu_custom_call" | custom-call | tf_op jit(solution)/shard_map/pallas_call | solution.py:452
  51.1 0.8 %slice_bitcast_fusion = (bf16[1,1,32,3072]{3,2,1,0:T(8,128)(2,1)}, bf16[1,1,32,3072]{3,2,1,0:T(8,128)(2,1)}, bf16[1,1,32,3072]{3,2,1,0:T(8,128)(2,1)}) fusion(bf16[3,32,3072]{2,1,0:T(8,128)(2,1)S(1)} %shard_map.85), kind=kLoop, calls=%fused_computation | loop fusion | bytes 1179648 | tf_op jit(solution)/shard_map/reshape;squeeze | solution.py:494

commit v6 on v5

--- a/solution.py
+++ b/solution.py
@@ -6,7 +6,7 @@
 from jax.sharding import PartitionSpec as P
 
 HD = 128
-ROUTES = (((0, 1), (0, 1), (0, 1)), ((0, 1), (0, 1), (0, 1)))
+ROUTES = (((0, 1), (0, 1), (0, 1)), ((0, 1), (0, 1), (0, 0)))
 MESH = pl.DeviceIdType.MESH
 F32 = jnp.float32
 BF16 = jnp.bfloat16
@@ -25,7 +25,7 @@
     xin, o_in, n_in, n_out, qd, kv, pad, st_out, st_in, st,
     k_t, dq_acc, kv_acc, rq_send, rq_recv, rk_send, rk_recv, out_send, relay, raw,
     sem_load, s_in, r_in, s_st, r_st, s_z, r_z, s_x, r_x, s_sz, r_sz,
-    s_rq, r_rq, s_rk, r_rk, s_out, r_out, s_relay, r_relay, s_raw, r_raw, s_spread,
+    s_rq, r_rq, s_rk, r_rk, s_out, s_out2, r_out, s_relay, r_relay, s_raw, r_raw, s_spread,
 ):
     ih, iw, me = lax.axis_index("ha"), lax.axis_index("wa"), lax.axis_index("hd")
     tile = nd * tok
@@ -290,84 +290,115 @@
             device_id={axis: other}, device_id_type=MESH,
         )
 
-    def out_copy(h, t):
-        d = lax.rem(me + 1 + t, nd)
-        return pltpu.make_async_remote_copy(
-            src_ref=out_send.at[h, :, pl.ds(pl.multiple_of(d * tok, tok), tok), :],
-            dst_ref=res.at[:, :, pl.ds(pl.multiple_of((h * nd + me) * HD, HD), HD)],
-            send_sem=s_out.at[h, t], recv_sem=r_out.at[h],
-            device_id={"hd": d}, device_id_type=MESH,
-        )
+    first_b = jnp.where(iw == mid, 2, 0)
+    last_b = 2 - first_b
+
+    def wait_columns(h, b):
+        for side in sides_w:
+            @pl.when(side[1] & (b == side[3]))
+            def _():
+                arrived(kv, side[3], h, r_x)
 
     def compute(h):
-        for side in sides_w:
-            when(side, lambda: arrived(kv, side[3], h, r_x))
-        for b in range(3):
-            k_t[b] = kv[b, h, 0].T
-        for n, a in enumerate((1, 0, 2)):
-            if a != 1:
-                side = sides_h[a // 2]
-                when(side, lambda: arrived(qd, a, h, r_z))
-
-                @pl.when(side[1] & (h == 0))
-                def _():
-                    pltpu.make_async_copy(st.at[a], st.at[a], r_sz.at[a // 2]).wait()
+        def pair(a, b, new_q, new_kv):
             q, g = qd[a, h, 0], qd[a, h, 1]
             norm = st[a, pl.ds(h, 1), :]
             dots = st[a, pl.ds(heads + h, 1), :]
-            dq = None
-            for b in range(3):
-                s_t = dot(kv[b, h, 0], q, NT)
-                p_t = jnp.exp(s_t * scale - norm)
-                dp_t = dot(kv[b, h, 1], g, NT)
-                ds_t = (p_t * (dp_t - dots) * scale).astype(BF16)
-                dk = dot(ds_t, q, NN)
-                dv = dot(p_t.astype(BF16), g, NN)
-                term = dot(k_t[b], ds_t, NN)
-                dq = term if dq is None else dq + term
-                if n == 0:
-                    kv_acc[h, b, 0] = dk
-                    kv_acc[h, b, 1] = dv
-                else:
-                    kv_acc[h, b, 0] += dk
-                    kv_acc[h, b, 1] += dv
-            if a == 1:
-                dq_acc[h] = dq
+            s_t = dot(kv[b, h, 0], q, NT)
+            p_t = jnp.exp(s_t * scale - norm)
+            dp_t = dot(kv[b, h, 1], g, NT)
+            ds_t = (p_t * (dp_t - dots) * scale).astype(BF16)
+            dk = dot(ds_t, q, NN)
+            dv = dot(p_t.astype(BF16), g, NN)
+            dq = dot(k_t[b], ds_t, NN)
+            if new_q:
+                dq_acc[h, a] = dq
             else:
-                rq_send[a // 2, h] = dq.astype(BF16)
-                when(sides_h[a // 2], lambda: back_q(h, sides_h[a // 2]).start())
-        for side in sides_w:
-            slot = side[3]
-            rk_send[slot // 2, h] = kv_acc[h, slot].astype(BF16)
-            send_kv(
-                h, side, rk_send.at[slot // 2, h], rk_recv.at[side[4] // 2, h],
-                s_rk.at[slot // 2, h], r_rk.at[side[4] // 2, h], 1,
-            )
+                dq_acc[h, a] += dq
+            if new_kv:
+                kv_acc[h, b, 0] = dk
+                kv_acc[h, b, 1] = dv
+            else:
+                kv_acc[h, b, 0] += dk
+                kv_acc[h, b, 1] += dv
+
+        def back_columns(b):
+            for side in sides_w:
+                slot = side[3]
+
+                @pl.when(b == slot)
+                def _():
+                    rk_send[slot // 2, h] = kv_acc[h, slot].astype(BF16)
+                    send_kv(
+                        h, side, rk_send.at[slot // 2, h], rk_recv.at[side[4] // 2, h],
+                        s_rk.at[slot // 2, h], r_rk.at[side[4] // 2, h], 1,
+                    )
+
+        def back_rows(a):
+            rq_send[a // 2, h] = dq_acc[h, a].astype(BF16)
+            when(sides_h[a // 2], lambda: back_q(h, sides_h[a // 2]).start())
+
+        k_t[1] = kv[1, h, 0].T
+        pair(1, 1, True, True)
+        wait_columns(h, first_b)
+        k_t[first_b] = kv[first_b, h, 0].T
+        pair(1, first_b, False, True)
+        for side in sides_h:
+            when(side, lambda: arrived(qd, side[3], h, r_z))
+
+            @pl.when(side[1] & (h == 0))
+            def _():
+                pltpu.make_async_copy(st.at[side[3]], st.at[side[3]], r_sz.at[side[3] // 2]).wait()
+        pair(0, first_b, True, False)
+        pair(2, first_b, True, False)
+        back_columns(first_b)
+        pair(0, 1, False, False)
+        pair(2, 1, False, False)
+        wait_columns(h, last_b)
+        k_t[last_b] = kv[last_b, h, 0].T
+        pair(0, last_b, False, True)
+        back_rows(0)
+        pair(2, last_b, False, False)
+        back_rows(2)
+        pair(1, last_b, False, False)
+        back_columns(last_b)
+
+    def out_copy(h, t, rows, sem):
+        d = lax.rem(me + 1 + t, nd)
+        return pltpu.make_async_remote_copy(
+            src_ref=out_send.at[h, rows, pl.ds(pl.multiple_of(d * tok, tok), tok), :],
+            dst_ref=res.at[rows, :, pl.ds(pl.multiple_of((h * nd + me) * HD, HD), HD)],
+            send_sem=sem.at[h, t], recv_sem=r_out.at[h],
+            device_id={"hd": d}, device_id_type=MESH,
+        )
+
+    def send_out(h, rows, sem):
+        def one(t, c):
+            out_copy(h, t, rows, sem).start()
+            return c
+
+        lax.fori_loop(0, nd - 1, one, 0)
+        pltpu.make_async_copy(
+            out_send.at[h, rows, my_rows, :],
+            res.at[rows, :, pl.ds(pl.multiple_of((h * nd + me) * HD, HD), HD)],
+            r_out.at[h],
+        ).start()
 
     def finish(h):
         for n, side in enumerate(sides_h):
             when(side, lambda: pltpu.make_async_copy(
                 rq_recv.at[n, h], rq_recv.at[n, h], r_rq.at[n, h]).wait())
+        dq = dq_acc[h, 1] + rq_recv[0, h].astype(F32) + rq_recv[1, h].astype(F32)
+        out_send[h, 0] = dq.T.astype(BF16)
+        send_out(h, pl.ds(0, 1), s_out)
         for n, side in enumerate(sides_w):
             when(side, lambda: pltpu.make_async_copy(
                 rk_recv.at[n, h], rk_recv.at[n, h], r_rk.at[n, h]).wait())
-        dq = dq_acc[h] + rq_recv[0, h].astype(F32) + rq_recv[1, h].astype(F32)
-        out_send[h, 0] = dq.T.astype(BF16)
         for n in range(2):
             out_send[h, 1 + n] = (
                 kv_acc[h, 1, n] + rk_recv[0, h, n].astype(F32) + rk_recv[1, h, n].astype(F32)
             ).astype(BF16)
-
-        def one(t, c):
-            out_copy(h, t).start()
-            return c
-
-        lax.fori_loop(0, nd - 1, one, 0)
-        pltpu.make_async_copy(
-            out_send.at[h, :, my_rows, :],
-            res.at[:, :, pl.ds(pl.multiple_of((h * nd + me) * HD, HD), HD)],
-            r_out.at[h],
-        ).start()
+        send_out(h, pl.ds(1, 2), s_out2)
 
     def step(h, c):
         compute(h)
@@ -393,8 +424,9 @@
             for part in range(2):
                 src = xin.at[pl.ds(2 * part, 2), :, pl.ds(0, HD)]
                 pltpu.make_async_copy(src, src, s_in.at[h, part, t]).wait()
-            src = out_send.at[h, :, pl.ds(0, tok), :]
-            pltpu.make_async_copy(src, src, s_out.at[h, t]).wait()
+            for rows, sem in ((pl.ds(0, 1), s_out), (pl.ds(1, 2), s_out2)):
+                src = out_send.at[h, rows, pl.ds(0, tok), :]
+                pltpu.make_async_copy(src, src, sem.at[h, t]).wait()
         src = st_out.at[pl.ds(0, 8), :]
         pltpu.make_async_copy(src, src, s_st.at[t]).wait()
         return c
@@ -466,7 +498,7 @@
                 pltpu.VMEM((nd, 8, 128), F32),
                 pltpu.VMEM((3, 8, tile), F32),
                 pltpu.VMEM((3, HD, tile), BF16),
-                pltpu.VMEM((heads, HD, tile), F32),
+                pltpu.VMEM((heads, 3, HD, tile), F32),
                 pltpu.VMEM((heads, 3, 2, tile, HD), F32),
                 pltpu.VMEM((2, heads, HD, tile), BF16),
                 pltpu.VMEM((2, heads, HD, tile), BF16),
@@ -483,7 +515,7 @@
                 dma((2,)), dma((2,)),
                 dma((2, heads)), dma((2, heads)),
                 dma((2, heads)), dma((2, heads)),
-                dma((heads, nd - 1)), dma((heads,)),
+                dma((heads, nd - 1)), dma((heads, nd - 1)), dma((heads,)),
                 dma((2, heads, 2)), dma((2, heads, 2)),
                 dma((2,)), dma((2,)), dma((2, nd - 1)),
             ],

time: 52.1 us -> 51.8 us (level)
    pallas_call x1, Pallas kernels: 50.5 us -> 50 us  [per_device(): pl.pallas_call(kernel, out_shape=pltpu.VMEM((3, tok, chan), BF16), in_spe...]
where the time goes in v6:
time: 51.8 us; the launch traced here: 51.4 us
  Pallas kernels  50 us (97%)
  local copies, waits for them, and re-layouts  0.82 us (2%)
  between operations  0.64 us (1%)
    pallas_call x1, Pallas kernels, per_device(): pl.pallas_call(kernel, out_shape=pltpu.VMEM((3, tok, chan), BF16), in_spe...  50 us

profile of v6, /device:TPU:71, one launch (start us, length us, event | category | flops | bytes accessed | tf_op | source)
XLA Modules:
  0.0 51.4 jit_solution(5855641130461174432)
XLA Ops:
  0.6 50.0 %shard_map.85 = bf16[3,32,3072]{2,1,0:T(8,128)(2,1)S(1)} custom-call(bf16[32,3072]{1,0:T(8,128)(2,1)} %bitcast.14, bf16[32,3072]{1,0:T(8,128)(2,1)} %bitcast.15, bf16[32,3072]{1,0:T(8,128)(2,1)} %bitcast.16, bf16[32,3072]{1,0:T(8,128)(2,1)} %bitcast.17, bf16[32,3072]{1,0:T(8,128)(2,1)} %bitcast.18, f32[24,32]{1,0:T(8,128)} %bitcast.19), custom_call_target="tpu_custom_call" | custom-call | tf_op jit(solution)/shard_map/pallas_call | solution.py:484
  50.6 0.8 %slice_bitcast_fusion = (bf16[1,1,32,3072]{3,2,1,0:T(8,128)(2,1)}, bf16[1,1,32,3072]{3,2,1,0:T(8,128)(2,1)}, bf16[1,1,32,3072]{3,2,1,0:T(8,128)(2,1)}) fusion(bf16[3,32,3072]{2,1,0:T(8,128)(2,1)S(1)} %shard_map.85), kind=kLoop, calls=%fused_computation | loop fusion | bytes 1179648 | tf_op jit(solution)/shard_map/reshape;squeeze | solution.py:526

commit v7 on v6

--- a/solution.py
+++ b/solution.py
@@ -6,7 +6,7 @@
 from jax.sharding import PartitionSpec as P
 
 HD = 128
-ROUTES = (((0, 1), (0, 1), (0, 1)), ((0, 1), (0, 1), (0, 0)))
+ROUTES = (((0, 1), (0, 1), (0, 1)), ((2, 3), (0, 1), (0, 0)))
 MESH = pl.DeviceIdType.MESH
 F32 = jnp.float32
 BF16 = jnp.bfloat16

time: 51.8 us -> 50.8 us (0.981)
  Pallas kernels: 50 us -> 48.9 us
    pallas_call x1, Pallas kernels: 50 us -> 48.9 us  [per_device(): pl.pallas_call(kernel, out_shape=pltpu.VMEM((3, tok, chan), BF16), in_spe...]
where the time goes in v7:
time: 50.8 us; the launch traced here: 50.4 us
  Pallas kernels  48.9 us (96%)
  local copies, waits for them, and re-layouts  0.82 us (2%)
  between operations  0.64 us (1%)
    pallas_call x1, Pallas kernels, per_device(): pl.pallas_call(kernel, out_shape=pltpu.VMEM((3, tok, chan), BF16), in_spe...  48.9 us

profile of v7, /device:TPU:71, one launch (start us, length us, event | category | flops | bytes accessed | tf_op | source)
XLA Modules:
  0.0 50.4 jit_solution(4522542882815137366)
XLA Ops:
  0.6 48.9 %shard_map.85 = bf16[3,32,3072]{2,1,0:T(8,128)(2,1)S(1)} custom-call(bf16[32,3072]{1,0:T(8,128)(2,1)} %bitcast.14, bf16[32,3072]{1,0:T(8,128)(2,1)} %bitcast.15, bf16[32,3072]{1,0:T(8,128)(2,1)} %bitcast.16, bf16[32,3072]{1,0:T(8,128)(2,1)} %bitcast.17, bf16[32,3072]{1,0:T(8,128)(2,1)} %bitcast.18, f32[24,32]{1,0:T(8,128)} %bitcast.19), custom_call_target="tpu_custom_call" | custom-call | tf_op jit(solution)/shard_map/pallas_call | solution.py:484
  49.6 0.8 %slice_bitcast_fusion = (bf16[1,1,32,3072]{3,2,1,0:T(8,128)(2,1)}, bf16[1,1,32,3072]{3,2,1,0:T(8,128)(2,1)}, bf16[1,1,32,3072]{3,2,1,0:T(8,128)(2,1)}) fusion(bf16[3,32,3072]{2,1,0:T(8,128)(2,1)S(1)} %shard_map.85), kind=kLoop, calls=%fused_computation | loop fusion | bytes 1179648 | tf_op jit(solution)/shard_map/reshape;squeeze | solution.py:526
